TPU v7x, 32 devices: a whole 2x2x4 slice. The times are simulated.
32 devices in a mesh: dp: 8 (over y, x, core), tensor: 4 (over z).
Axes of the slice: x: 2, y: 2, z: 4, core: 2. Of those that a mesh axis runs over, the one named last changes fastest.
Arguments:
- tokens: bfloat16 [48, 256, 768], P('dp', 'tensor'), may hold values from -6 to 6
- cotangent: bfloat16 [48, 256, 768], P('dp', 'tensor'), may hold values from -6 to 6
- task_ids: int32 [48, 2], P('dp'), may hold values from 0 to 7
- key_mask: int32 [48, 256], P('dp'), may hold values from 0 to 1, as said below
- prompts: bfloat16 [2, 8, 50, 768], replicated, may hold values from -6 to 6
- norm_gain: bfloat16 [2, 2, 768], replicated, may hold values from 0.099609375 to 1.8984375
- norm_bias: bfloat16 [2, 2, 768], replicated, may hold values from -4 to 4
- qkv_weight: bfloat16 [2, 768, 2304], P(None, None, 'tensor'), may hold values from -0.21875 to 0.21875
- qv_bias: bfloat16 [2, 1536], P(None, 'tensor'), may hold values from -4 to 4
- out_weight: bfloat16 [2, 768, 768], P(None, 'tensor'), may hold values from -0.625 to 0.625
- branch_bias: bfloat16 [2, 2, 768], replicated, may hold values from -4 to 4
- up_weight: bfloat16 [2, 768, 3072], P(None, None, 'tensor'), may hold values from -0.21875 to 0.21875
- up_bias: bfloat16 [2, 3072], P(None, 'tensor'), may hold values from -4 to 4
- down_weight: bfloat16 [2, 3072, 768], P(None, 'tensor'), may hold values from -0.109375 to 0.109375
Outputs:
- out: bfloat16 [48, 256, 768], P('dp', 'tensor')
- grad_tokens: bfloat16 [48, 256, 768], P('dp', 'tensor')
- grad_prompts: float32 [2, 8, 50, 768], P(None, 'dp', None, 'tensor')
- grad_norm_gain: float32 [2, 2, 768], P(None, None, 'tensor')
- grad_norm_bias: float32 [2, 2, 768], P(None, None, 'tensor')
- grad_qkv_weight: float32 [2, 768, 2304], P(None, None, 'tensor')
- grad_qv_bias: float32 [2, 1536], P(None, 'tensor')
- grad_out_weight: float32 [2, 768, 768], P(None, 'tensor')
- grad_branch_bias: float32 [2, 2, 768], P(None, None, 'tensor')
- grad_up_weight: float32 [2, 768, 3072], P(None, None, 'tensor')
- grad_up_bias: float32 [2, 3072], P(None, 'tensor')
- grad_down_weight: float32 [2, 3072, 768], P(None, 'tensor')
Inputs may be any that keep to these rules, and one draw needn't show every extreme that they name: `key_mask`: each image's rows are 1 for its first 51 + n rows and 0 after, with 98 <= n <= 196; the first image has n = 196.
All inputs are finite; a program needn't handle non-finite values.
Results may differ from a plain program's by a relative error of at most 0.025.
Values may be sent and summed in bfloat16 or wider, within the bound.
No kernel may reach another device: no remote copies, remote signals or barrier semaphores. Data moves between devices by JAX's collectives and lax.ppermute only.
A program may use at most 192 MiB of HBM per device.

v0:
```python
import jax
import jax.numpy as jnp
from jax import lax
from jax.sharding import PartitionSpec as P

HEAD_DIM = 64
LAYERS = 2
PROMPTS = 50


epsilon = 1e-06
highest = lax.Precision.HIGHEST


def layer_norm(tok_rows, gain_vec, shift_vec):
    centre = tok_rows - jnp.mean(tok_rows, axis=-1, keepdims=True)
    spread = jnp.mean(centre * centre, axis=-1, keepdims=True)
    return centre * lax.rsqrt(spread + epsilon) * gain_vec + shift_vec


def smooth_gate(pre_act):
    return jax.nn.gelu(pre_act, approximate=False)


def product(einsum_form, left_op, right_op):
    return jnp.einsum(einsum_form, left_op, right_op, preferred_element_type=jnp.float32)


def per_device(
    tokens,
    cotangent,
    task_ids,
    key_mask,
    prompts,
    norm_gain,
    norm_bias,
    qkv_weight,
    qv_bias,
    out_weight,
    branch_bias,
    up_weight,
    up_bias,
    down_weight,
):
    images, rows_local, model_width = tokens.shape
    seq_rows = rows_local * lax.axis_size("tensor")
    heads_local = qkv_weight.shape[2] // (3 * HEAD_DIM)
    inner_width = heads_local * HEAD_DIM
    task_count = prompts.shape[1]
    score_scale = HEAD_DIM ** (-0.5)
    row_start = lax.axis_index("tensor") * rows_local
    positions = row_start + jnp.arange(rows_local)
    prompt_here = ((positions >= 1) & (positions <= PROMPTS))[None, :, None]
    valid_keys = (key_mask > 0)[:, None, None, :]
    row_mask = lax.dynamic_slice_in_dim(key_mask, row_start, rows_local, 1).astype(jnp.float32)[
        :, :, None
    ]
    gain_all = norm_gain.astype(jnp.float32)
    shifts = norm_bias.astype(jnp.float32)
    biases = branch_bias.astype(jnp.float32)
    pair_all = qv_bias.astype(jnp.float32).reshape(LAYERS, heads_local, 2, HEAD_DIM)
    up_shift = up_bias.astype(jnp.float32)
    task_hots = [
        (task_ids[:, layer_idx][:, None] == jnp.arange(task_count)[None, :]).astype(jnp.bfloat16)
        for layer_idx in range(LAYERS)
    ]

    def score_rows(query_rows, key_rows):
        raw_scores = product("iqhe,ikhe->ihqk", query_rows, key_rows)
        return jnp.where(valid_keys, raw_scores, -1000000000.0)

    tok_rows = tokens.astype(jnp.float32)
    kept_all = []
    for layer_idx in range(LAYERS):
        forward_tok_rows = tok_rows
        chosen = product(
            "it,tf->if",
            task_hots[layer_idx],
            prompts[layer_idx].reshape(task_count, PROMPTS * model_width),
        )
        placed = jnp.pad(
            chosen.reshape(images, PROMPTS, model_width),
            ((0, 0), (1, seq_rows - 1 - PROMPTS), (0, 0)),
        )
        placed = lax.dynamic_slice_in_dim(placed, row_start, rows_local, 1)
        forward_tok_rows = jnp.where(prompt_here, placed, forward_tok_rows)
        normed = layer_norm(forward_tok_rows, gain_all[layer_idx, 0], shifts[layer_idx, 0]).astype(
            jnp.bfloat16
        )
        forward_first_in = lax.all_gather(normed, "tensor", axis=1, tiled=True)
        qkv_all = product(
            "isd,dhce->ishce",
            forward_first_in,
            qkv_weight[layer_idx].reshape(model_width, heads_local, 3, HEAD_DIM),
        )
        pair_bias = pair_all[layer_idx]
        forward_query_rows = ((qkv_all[:, :, :, 0] + pair_bias[:, 0]) * score_scale).astype(
            jnp.bfloat16
        )
        forward_key_rows = qkv_all[:, :, :, 1].astype(jnp.bfloat16)
        forward_value_rows = (qkv_all[:, :, :, 2] + pair_bias[:, 1]).astype(jnp.bfloat16)
        scores = score_rows(forward_query_rows, forward_key_rows)
        row_peak = jnp.max(scores, axis=-1, keepdims=True)
        exp_scores = jnp.exp(scores - row_peak)
        totals = jnp.sum(exp_scores, axis=-1, keepdims=True)
        attn_probs = (exp_scores / totals).astype(jnp.bfloat16)
        forward_log_total = row_peak + jnp.log(totals)
        forward_mixed_heads = (
            product("ihqk,ikhe->iqhe", attn_probs, forward_value_rows)
            .reshape(images, seq_rows, inner_width)
            .astype(jnp.bfloat16)
        )
        attn_out = lax.psum_scatter(
            product("isc,cd->isd", forward_mixed_heads, out_weight[layer_idx]).astype(jnp.bfloat16),
            "tensor",
            scatter_dimension=1,
            tiled=True,
        ).astype(jnp.float32)
        forward_middle = forward_tok_rows + (attn_out + biases[layer_idx, 0])
        second = layer_norm(forward_middle, gain_all[layer_idx, 1], shifts[layer_idx, 1]).astype(
            jnp.bfloat16
        )
        forward_second_in = lax.all_gather(second, "tensor", axis=1, tiled=True)
        forward_hidden = (
            product("isd,df->isf", forward_second_in, up_weight[layer_idx]) + up_shift[layer_idx]
        )
        forward_active = smooth_gate(forward_hidden).astype(jnp.bfloat16)
        branch = lax.psum_scatter(
            product("isf,fd->isd", forward_active, down_weight[layer_idx]).astype(jnp.bfloat16),
            "tensor",
            scatter_dimension=1,
            tiled=True,
        ).astype(jnp.float32)
        result = forward_middle + (branch + biases[layer_idx, 1])
        forward_kept_set = (
            forward_tok_rows,
            forward_middle,
            forward_first_in,
            forward_query_rows,
            forward_key_rows,
            forward_value_rows,
            forward_log_total,
            forward_mixed_heads,
            forward_second_in,
            forward_hidden,
            forward_active,
        )
        tok_rows = result
        kept_all.append(forward_kept_set)
    out_rows = (tok_rows * row_mask).astype(jnp.bfloat16)
    grad_rows = cotangent.astype(jnp.float32) * row_mask
    pieces = []
    for layer_idx in reversed(range(LAYERS)):
        backward_kept_set = kept_all[layer_idx]
        (
            backward_tok_rows,
            middle,
            first_in,
            backward_query_rows,
            backward_key_rows,
            value_rows,
            log_total,
            mixed_heads,
            second_in,
            hidden,
            active,
        ) = backward_kept_set
        bias_mlp = jnp.sum(grad_rows, axis=(0, 1))
        down_in = lax.all_gather(grad_rows.astype(jnp.bfloat16), "tensor", axis=1, tiled=True)
        backward_grad_down = product("isf,isd->fd", active, down_in)
        grad_active = product("isd,fd->isf", down_in, down_weight[layer_idx])
        grad_hidden = jax.vjp(smooth_gate, hidden)[1](grad_active)[0].astype(jnp.bfloat16)
        backward_grad_upb = jnp.sum(grad_hidden.astype(jnp.float32), axis=(0, 1))
        backward_grad_up = product("isd,isf->df", second_in, grad_hidden)
        back_two = lax.psum_scatter(
            product("isf,df->isd", grad_hidden, up_weight[layer_idx]).astype(jnp.bfloat16),
            "tensor",
            scatter_dimension=1,
            tiled=True,
        ).astype(jnp.float32)
        norm_two = jax.vjp(layer_norm, middle, gain_all[layer_idx, 1], shifts[layer_idx, 1])[1]
        grad_mid, gain_two, shift_two = norm_two(back_two)
        grad_mid = grad_rows + grad_mid
        bias_attn = jnp.sum(grad_mid, axis=(0, 1))
        attn_in = lax.all_gather(grad_mid.astype(jnp.bfloat16), "tensor", axis=1, tiled=True)
        backward_grad_outw = product("isc,isd->cd", mixed_heads, attn_in)
        grad_mixed = (
            product("isd,cd->isc", attn_in, out_weight[layer_idx])
            .astype(jnp.bfloat16)
            .reshape(images, seq_rows, heads_local, HEAD_DIM)
        )
        probs_full = jnp.exp(score_rows(backward_query_rows, backward_key_rows) - log_total)
        probs_low = probs_full.astype(jnp.bfloat16)
        grad_value = product("ihqk,iqhe->ikhe", probs_low, grad_mixed).astype(jnp.bfloat16)
        grad_probs = product("iqhe,ikhe->ihqk", grad_mixed, value_rows)
        grad_scores = (
            probs_full * (grad_probs - jnp.sum(probs_full * grad_probs, axis=-1, keepdims=True))
        ).astype(jnp.bfloat16)
        grad_query = product("ihqk,ikhe->iqhe", grad_scores, backward_key_rows).astype(
            jnp.bfloat16
        ) * jnp.bfloat16(score_scale)
        grad_key = product("ihqk,iqhe->ikhe", grad_scores, backward_query_rows).astype(jnp.bfloat16)
        grad_qkv = jnp.stack([grad_query, grad_key, grad_value], axis=3).reshape(
            images, seq_rows, 3 * inner_width
        )
        backward_grad_qkvw = product("isd,isc->dc", first_in, grad_qkv)
        backward_grad_pair = jnp.stack(
            [
                jnp.sum(grad_query.astype(jnp.float32), axis=(0, 1)),
                jnp.sum(grad_value.astype(jnp.float32), axis=(0, 1)),
            ],
            axis=1,
        ).reshape(2 * inner_width)
        back_one = lax.psum_scatter(
            product("isc,dc->isd", grad_qkv, qkv_weight[layer_idx]).astype(jnp.bfloat16),
            "tensor",
            scatter_dimension=1,
            tiled=True,
        ).astype(jnp.float32)
        norm_one = jax.vjp(
            layer_norm, backward_tok_rows, gain_all[layer_idx, 0], shifts[layer_idx, 0]
        )[1]
        grad_in, gain_one, shift_one = norm_one(back_one)
        grad_in = grad_mid + grad_in
        holder = lax.dynamic_update_slice_in_dim(
            jnp.zeros((images, seq_rows, model_width), jnp.float32), grad_in, row_start, 1
        )
        picked = holder[:, 1 : 1 + PROMPTS].reshape(images, PROMPTS * model_width)
        backward_prompt_part = jnp.einsum(
            "it,if->tf", task_hots[layer_idx].astype(jnp.float32), picked, precision=highest
        )
        grad_in = jnp.where(prompt_here, 0.0, grad_in)
        backward_small_grads = jnp.stack(
            [gain_one, gain_two, shift_one, shift_two, bias_attn, bias_mlp]
        )
        grad_rows = grad_in
        layer_parts = (
            backward_grad_qkvw,
            backward_grad_pair,
            backward_grad_outw,
            backward_grad_up,
            backward_grad_upb,
            backward_grad_down,
            backward_small_grads,
            backward_prompt_part.reshape(task_count, PROMPTS, model_width),
        )
        pieces.append(layer_parts)
    ordered = list(reversed(pieces))
    collected = [jnp.stack(group_list) for group_list in zip(*ordered)]
    grad_qkvw, grad_pair, grad_outw, grad_up, grad_upb, grad_down, small_grads, prompt_part = (
        collected
    )
    small_grads = lax.psum_scatter(
        small_grads.astype(jnp.bfloat16), "tensor", scatter_dimension=2, tiled=True
    ).astype(jnp.float32)
    summed = lax.psum(
        (grad_qkvw, grad_pair, grad_outw, grad_up, grad_upb, grad_down, small_grads), "dp"
    )
    by_task = lax.psum_scatter(prompt_part, "dp", scatter_dimension=1, tiled=True)
    prompt_grad = lax.psum_scatter(
        by_task.astype(jnp.bfloat16), "tensor", scatter_dimension=3, tiled=True
    ).astype(jnp.float32)
    grad_qkvw, grad_pair, grad_outw, grad_up, grad_upb, grad_down, small_grads = summed
    small_grads = small_grads.reshape(LAYERS, 3, 2, small_grads.shape[2])
    return (
        out_rows,
        grad_rows.astype(jnp.bfloat16),
        prompt_grad,
        small_grads[:, 0],
        small_grads[:, 1],
        grad_qkvw,
        grad_pair,
        grad_outw,
        small_grads[:, 2],
        grad_up,
        grad_upb,
        grad_down,
    )


def solution(mesh):
    placed = (
        P("dp", "tensor", None),
        P("dp", "tensor", None),
        P("dp", None),
        P("dp", None),
        P(),
        P(),
        P(),
        P(None, None, "tensor"),
        P(None, "tensor"),
        P(None, "tensor", None),
        P(),
        P(None, None, "tensor"),
        P(None, "tensor"),
        P(None, "tensor", None),
    )
    return jax.shard_map(
        per_device,
        mesh=mesh,
        in_specs=placed,
        out_specs=(
            P("dp", "tensor", None),
            P("dp", "tensor", None),
            P(None, "dp", None, "tensor"),
            P(None, None, "tensor"),
            P(None, None, "tensor"),
            P(None, None, "tensor"),
            P(None, "tensor"),
            P(None, "tensor", None),
            P(None, None, "tensor"),
            P(None, None, "tensor"),
            P(None, "tensor"),
            P(None, "tensor", None),
        ),
        check_vma=False,
    )
```

profile of v0, /device:TPU:0, one launch (start us, length us, event | category | flops | bytes accessed | tf_op | source)
XLA Modules:
  0.0 1278.1 jit_solution(17915991943008869448)
XLA Ops:
  15.0 51.1 %all-gather.9.cloned.1.call-done = bf16[6,256,768]{2,1,0:T(8,128)(2,1)} async-done(((bf16[6,64,768]{2,1,0:T(8,128)(2,1)}), bf16[6,256,768]{2,1,0:T(8,128)(2,1)}) %all-gather.9.cloned.1.call-update) | async-done | bytes 2359312 | tf_op jit(solution)/shard_map/all_gather | solution.py:90
  78.1 46.3 %reduce-scatter.12.cloned.1.call-done = bf16[6,64,768]{2,1,0:T(8,128)(2,1)} async-done(((bf16[6,256,768]{2,1,0:T(8,128)(2,1)}), bf16[6,64,768]{2,1,0:T(8,128)(2,1)}) %reduce-scatter.12.cloned.1.call-update) | async-done | bytes 589840 | tf_op jit(solution)/shard_map/reduce_scatter | solution.py:113
  128.0 49.2 %all-gather.11.cloned.1.call-done = bf16[6,256,768]{2,1,0:T(8,128)(2,1)} async-done(((bf16[6,64,768]{2,1,0:T(8,128)(2,1)}), bf16[6,256,768]{2,1,0:T(8,128)(2,1)}) %all-gather.11.cloned.1.call-update) | async-done | bytes 2359312 | tf_op jit(solution)/shard_map/all_gather | solution.py:123
  177.2 5.2 fusion.86
  182.5 11.7 multiply_convert_fusion.3
  201.8 44.3 %reduce-scatter.14.cloned.1.call-done = bf16[6,64,768]{2,1,0:T(8,128)(2,1)} async-done(((bf16[6,256,768]{2,1,0:T(8,128)(2,1)}), bf16[6,64,768]{2,1,0:T(8,128)(2,1)}) %reduce-scatter.14.cloned.1.call-update) | async-done | bytes 589840 | tf_op jit(solution)/shard_map/reduce_scatter | solution.py:128
  253.2 47.0 %all-gather.13.cloned.1.call-done = bf16[6,256,768]{2,1,0:T(8,128)(2,1)} async-done(((bf16[6,64,768]{2,1,0:T(8,128)(2,1)}), bf16[6,256,768]{2,1,0:T(8,128)(2,1)}) %all-gather.13.cloned.1.call-update) | async-done | bytes 2359312 | tf_op jit(solution)/shard_map/all_gather | solution.py:90
  312.2 46.6 %reduce-scatter.16.cloned.1.call-done = bf16[6,64,768]{2,1,0:T(8,128)(2,1)} async-done(((bf16[6,256,768]{2,1,0:T(8,128)(2,1)}), bf16[6,64,768]{2,1,0:T(8,128)(2,1)}) %reduce-scatter.16.cloned.1.call-update) | async-done | bytes 589840 | tf_op jit(solution)/shard_map/reduce_scatter | solution.py:113
  366.3 46.6 %all-gather.15.cloned.1.call-done = bf16[6,256,768]{2,1,0:T(8,128)(2,1)} async-done(((bf16[6,64,768]{2,1,0:T(8,128)(2,1)}), bf16[6,256,768]{2,1,0:T(8,128)(2,1)}) %all-gather.15.cloned.1.call-update) | async-done | bytes 2359312 | tf_op jit(solution)/shard_map/all_gather | solution.py:123
  412.9 5.2 fusion.87
  420.3 11.8 multiply_convert_fusion.2
  432.0 32.3 %all-gather.17.cloned.1.call-done = bf16[6,256,768]{2,1,0:T(8,128)(2,1)} async-done(((bf16[6,64,768]{2,1,0:T(8,128)(2,1)}), bf16[6,256,768]{2,1,0:T(8,128)(2,1)}) %all-gather.17.cloned.1.call-update) | async-done | bytes 2359312 | tf_op jit(solution)/shard_map/all_gather | solution.py:169
  464.3 8.9 convert_reduce_fusion
  478.3 5.4 convolution_convert_fusion.4
  483.8 41.3 %reduce-scatter.20.cloned.1.call-done = bf16[6,64,768]{2,1,0:T(8,128)(2,1)} async-done(((bf16[6,256,768]{2,1,0:T(8,128)(2,1)}), bf16[6,64,768]{2,1,0:T(8,128)(2,1)}) %reduce-scatter.20.cloned.1.call-update) | async-done | bytes 589840 | tf_op jit(solution)/shard_map/reduce_scatter | solution.py:175
  530.7 44.2 %reduce-scatter.18.cloned.1.call-done = bf16[6,64,768]{2,1,0:T(8,128)(2,1)} async-done(((bf16[6,256,768]{2,1,0:T(8,128)(2,1)}), bf16[6,64,768]{2,1,0:T(8,128)(2,1)}) %reduce-scatter.18.cloned.1.call-update) | async-done | bytes 589840 | tf_op jit(solution)/shard_map/reduce_scatter | solution.py:128
  582.2 48.7 %all-gather.19.cloned.1.call-done = bf16[6,256,768]{2,1,0:T(8,128)(2,1)} async-done(((bf16[6,64,768]{2,1,0:T(8,128)(2,1)}), bf16[6,256,768]{2,1,0:T(8,128)(2,1)}) %all-gather.19.cloned.1.call-update) | async-done | bytes 2359312 | tf_op jit(solution)/shard_map/all_gather | solution.py:185
  633.5 4.5 multiply_reduce_fusion.1
  650.2 47.0 %reduce-scatter.22.cloned.1.call-done = bf16[6,64,768]{2,1,0:T(8,128)(2,1)} async-done(((bf16[6,256,768]{2,1,0:T(8,128)(2,1)}), bf16[6,64,768]{2,1,0:T(8,128)(2,1)}) %reduce-scatter.22.cloned.1.call-update) | async-done | bytes 589840 | tf_op jit(solution)/shard_map/reduce_scatter | solution.py:214
  706.0 49.6 %all-gather.21.cloned.1.call-done = bf16[6,256,768]{2,1,0:T(8,128)(2,1)} async-done(((bf16[6,64,768]{2,1,0:T(8,128)(2,1)}), bf16[6,256,768]{2,1,0:T(8,128)(2,1)}) %all-gather.21.cloned.1.call-update) | async-done | bytes 2359312 | tf_op jit(solution)/shard_map/all_gather | solution.py:169
  755.6 8.9 convert_reduce_fusion.1
  769.5 47.0 %reduce-scatter.24.cloned.1.call-done = bf16[6,64,768]{2,1,0:T(8,128)(2,1)} async-done(((bf16[6,256,768]{2,1,0:T(8,128)(2,1)}), bf16[6,64,768]{2,1,0:T(8,128)(2,1)}) %reduce-scatter.24.cloned.1.call-update) | async-done | bytes 589840 | tf_op jit(solution)/shard_map/reduce_scatter | solution.py:175
  826.7 49.4 %all-gather.23.cloned.1.call-done = bf16[6,256,768]{2,1,0:T(8,128)(2,1)} async-done(((bf16[6,64,768]{2,1,0:T(8,128)(2,1)}), bf16[6,256,768]{2,1,0:T(8,128)(2,1)}) %all-gather.23.cloned.1.call-update) | async-done | bytes 2359312 | tf_op jit(solution)/shard_map/all_gather | solution.py:185
  878.7 4.5 multiply_reduce_fusion
  895.6 6.0 convolution_bitcast_fusion
  913.1 4.5 convolution_bitcast_fusion.4
  917.9 4.6 convolution_bitcast_fusion.1
  938.9 4.4 convolution_bitcast_fusion.5
  954.9 11.6 reduce-scatter.28.cloned.1.call-done
  967.5 59.2 %all-reduce.13 = (bf16[2,8,50,768]{3,0,2,1:T(2,128)(2,1)}, f32[2,3,2,192]{3,0,2,1:T(2,128)S(1)}, f32[2,384]{1,0:T(2,128)}, f32[2,768]{1,0:T(2,128)}) all-reduce(f32[2,8,50,768]{3,0,2,1:T(2,128)} %copy.249, f32[2,3,2,192]{3,0,2,1:T(2,128)S(1)} %bitcast.325, ...), channel_id=10, replica_groups=mesh['dp'=8,'tensor'=4] {'dp'}, use_global_device_ids=true, to_apply=%region_30.31.clone | all-reduce | flops 619008 | bytes 3723264
  1038.1 27.0 %all-reduce.10.cloned.1.call-done = bf16[2,1,50,768]{2,0,1,3:T(2,128)(2,1)} async-done(((bf16[2,1,50,768]{2,0,1,3:T(2,128)(2,1)}), bf16[2,1,50,768]{2,0,1,3:T(2,128)(2,1)}) %all-reduce.10.cloned.1.call-update) | async-done | bytes 153616
  1066.8 193.7 %all-reduce.12.cloned.1.call-done = (f32[2,768,576]{1,2,0:T(8,128)}, f32[2,192,768]{2,1,0:T(8,128)}, f32[2,768,768]{2,1,0:T(8,128)}, f32[2,768,768]{2,1,0:T(8,128)}) async-done(((f32[2,768,576]{1,2,0:T(8,128)}, f32[2,192,768]{2,1,0:T(8,128)}, f32[2,768,768]{2,1,0:T(8,128)}, f32[2,768,768]{2,1,0:T(8,128)}), (f32[2,768,576]{1,2,0:T(8,128)}, f32[2,192,768]{2,1,0:T(8,128)}, f32[2,768,768]{2,1,0:T(8,128)}, ...) | async-done | bytes 14155792 | tf_op jit(solution)/shard_map/psum | solution.py:256
  (475 shorter events, 193.8 us)
Async XLA Ops:
  7.2 59.0 %all-gather.9.cloned.1.call-start = ((), (), s32[]{:S(2)}) async-start(), calls=%async_computation.9 | async-start | bytes 2949120 | tf_op jit(solution)/shard_map/all_gather | solution.py:90
  7.3 238.9 %copy-start.83 = (pred[64]{0:T(512)(128)(4,1)}, pred[64]{0:T(512)(128)(4,1)S(1)}, u32[]{:S(2)}) copy-start(pred[64]{0:T(512)(128)(4,1)S(1)} %compare_and_fusion) | copy-start | bytes 196
  8.0 191.1 %copy-start.117 = (s32[6]{0:T(128)}, s32[6]{0:T(128)S(1)}, u32[]{:S(2)}) copy-start(s32[6]{0:T(128)S(1)} %get-tuple-element.140) | copy-start | bytes 76
  11.8 114.3 %copy-start.58 = (f32[768]{0:T(1024)}, f32[768]{0:T(1024)S(1)}, u32[]{:S(2)}) copy-start(f32[768]{0:T(1024)S(1)} %get-tuple-element.165) | copy-start | bytes 9220
  12.9 111.6 %reduce-scatter.12.cloned.1.call-start = ((), (), s32[]{:S(2)}) async-start(), calls=%async_computation.10 | async-start | bytes 2949120 | tf_op jit(solution)/shard_map/reduce_scatter | solution.py:113
  13.6 56.0 %copy-start.87 = (f32[3,64]{1,0:T(4,128)}, f32[3,64]{1,0:T(4,128)S(1)}, u32[]{:S(2)}) copy-start(f32[3,64]{1,0:T(4,128)S(1)} %get-tuple-element.168) | copy-start | bytes 2308
  13.6 58.0 %copy-start.101 = (f32[3,64]{1,0:T(4,128)}, f32[3,64]{1,0:T(4,128)S(1)}, u32[]{:S(2)}) copy-start(f32[3,64]{1,0:T(4,128)S(1)} %get-tuple-element.169) | copy-start | bytes 2308
  77.4 99.8 %all-gather.11.cloned.1.call-start = ((), (), s32[]{:S(2)}) async-start(), calls=%async_computation.11 | async-start | bytes 2949120 | tf_op jit(solution)/shard_map/all_gather | solution.py:123
  126.0 56.4 %copy-start.78 = (f32[6,64]{1,0:T(8,128)}, f32[6,64]{1,0:T(8,128)S(1)}, u32[]{:S(2)}) copy-start(f32[6,64]{1,0:T(8,128)S(1)} %multiply_reduce_fusion.4) | copy-start | bytes 4612
  126.0 56.4 %copy-start.68 = (f32[6,64]{1,0:T(8,128)}, f32[6,64]{1,0:T(8,128)S(1)}, u32[]{:S(2)}) copy-start(f32[6,64]{1,0:T(8,128)S(1)} %fusion.141) | copy-start | bytes 4612
  127.1 119.0 %reduce-scatter.14.cloned.1.call-start = ((), (), s32[]{:S(2)}) async-start(), calls=%async_computation.12 | async-start | bytes 2949120 | tf_op jit(solution)/shard_map/reduce_scatter | solution.py:128
  128.0 54.4 %copy-start.93 = (f32[768]{0:T(1024)}, f32[768]{0:T(1024)S(1)}, u32[]{:S(2)}) copy-start(f32[768]{0:T(1024)S(1)} %get-tuple-element.97) | copy-start | bytes 9220
  199.1 101.2 %all-gather.13.cloned.1.call-start = ((), (), s32[]{:S(2)}) async-start(), calls=%async_computation.13 | async-start | bytes 2949120 | tf_op jit(solution)/shard_map/all_gather | solution.py:90
  250.5 108.3 %reduce-scatter.16.cloned.1.call-start = ((), (), s32[]{:S(2)}) async-start(), calls=%async_computation.14 | async-start | bytes 2949120 | tf_op jit(solution)/shard_map/reduce_scatter | solution.py:113
  311.7 101.1 %all-gather.15.cloned.1.call-start = ((), (), s32[]{:S(2)}) async-start(), calls=%async_computation.15 | async-start | bytes 2949120 | tf_op jit(solution)/shard_map/all_gather | solution.py:123
  362.8 101.6 %all-gather.17.cloned.1.call-start = ((), (), s32[]{:S(2)}) async-start(), calls=%async_computation.17 | async-start | bytes 2949120 | tf_op jit(solution)/shard_map/all_gather | solution.py:169
  366.2 158.9 %reduce-scatter.20.cloned.1.call-start = ((), (), s32[]{:S(2)}) async-start(), calls=%async_computation.18 | async-start | bytes 2949120 | tf_op jit(solution)/shard_map/reduce_scatter | solution.py:175
  478.1 96.8 %reduce-scatter.18.cloned.1.call-start = ((), (), s32[]{:S(2)}) async-start(), calls=%async_computation.16 | async-start | bytes 2949120 | tf_op jit(solution)/shard_map/reduce_scatter | solution.py:128
  483.8 147.1 %all-gather.19.cloned.1.call-start = ((), (), s32[]{:S(2)}) async-start(), calls=%async_computation.19 | async-start | bytes 2949120 | tf_op jit(solution)/shard_map/all_gather | solution.py:185
  580.7 116.5 %reduce-scatter.22.cloned.1.call-start = ((), (), s32[]{:S(2)}) async-start(), calls=%async_computation.20 | async-start | bytes 2949120 | tf_op jit(solution)/shard_map/reduce_scatter | solution.py:214
  650.2 105.4 %all-gather.21.cloned.1.call-start = ((), (), s32[]{:S(2)}) async-start(), calls=%async_computation.21 | async-start | bytes 2949120 | tf_op jit(solution)/shard_map/all_gather | solution.py:169
  703.5 52.1 %copy-start.94 = (f32[768]{0:T(1024)S(1)}, f32[768]{0:T(1024)}, u32[]{:S(2)}) copy-start(f32[768]{0:T(1024)} %copy-done.93) | copy-start | bytes 9220
  705.5 111.0 %reduce-scatter.24.cloned.1.call-start = ((), (), s32[]{:S(2)}) async-start(), calls=%async_computation.22 | async-start | bytes 2949120 | tf_op jit(solution)/shard_map/reduce_scatter | solution.py:175
  769.4 48.5 %copy-start.69 = (f32[6,64]{1,0:T(8,128)S(1)}, f32[6,64]{1,0:T(8,128)}, u32[]{:S(2)}) copy-start(f32[6,64]{1,0:T(8,128)} %copy-done.68) | copy-start | bytes 4612
  769.5 106.6 %all-gather.23.cloned.1.call-start = ((), (), s32[]{:S(2)}) async-start(), calls=%async_computation.23 | async-start | bytes 2949120 | tf_op jit(solution)/shard_map/all_gather | solution.py:185
  825.0 51.0 %copy-start.43 = (bf16[2,192,768]{2,1,0:T(8,128)(2,1)S(1)}, bf16[2,192,768]{2,1,0:T(8,128)(2,1)}, u32[]{:S(2)}) copy-start(bf16[2,192,768]{2,1,0:T(8,128)(2,1)} %param.23) | copy-start | bytes 1769476
  825.9 52.7 %copy-start.102 = (f32[3,64]{1,0:T(4,128)S(1)}, f32[3,64]{1,0:T(4,128)}, u32[]{:S(2)}) copy-start(f32[3,64]{1,0:T(4,128)} %copy-done.101) | copy-start | bytes 2308
  825.9 117.4 %reduce-scatter.26.cloned.1.call-start = ((), (), s32[]{:S(2)}) async-start(), calls=%async_computation.24 | async-start | bytes 2949120 | tf_op jit(solution)/shard_map/reduce_scatter | solution.py:214
  895.3 71.2 %reduce-scatter.28.cloned.1.call-start = ((), (), s32[]{:S(2)}) async-start(), calls=%async_computation.25 | async-start | bytes 245760
  948.2 116.9 %all-reduce.10.cloned.1.call-start = ((), (), s32[]{:S(2)}) async-start(), calls=%async_computation.26 | async-start | bytes 786432
  954.9 74.8 %copy-start.32 = (f32[1,768,576]{1,2,0:T(8,128)S(1)}, f32[1,768,576]{1,2,0:T(8,128)}, u32[]{:S(2)}) copy-start(f32[1,768,576]{1,2,0:T(8,128)} %convolution_bitcast_fusion.4) | copy-start | bytes 5308420
  1029.7 230.9 %all-reduce.12.cloned.1.call-start = ((), (), s32[]{:S(2)}) async-start(), calls=%async_computation.27 | async-start | bytes 28311552 | tf_op jit(solution)/shard_map/psum | solution.py:256
  (121 other events, 482.9 us)
Sparse Core Ops, SparseCore 0:
  13.0 53.1 all-gather.8
  77.5 46.8 reduce-scatter.11
  127.3 49.9 all-gather.10
  199.2 46.8 reduce-scatter.13
  250.6 49.5 all-gather.12
  311.8 46.8 reduce-scatter.15
  362.9 49.9 all-gather.14
  415.0 49.2 all-gather.16
  478.2 46.8 reduce-scatter.19
  527.3 47.5 reduce-scatter.17
  580.9 49.9 all-gather.18
  650.3 46.8 reduce-scatter.21
  705.6 49.9 all-gather.20
  769.6 46.8 reduce-scatter.23
  826.1 49.9 all-gather.22
  895.5 46.8 reduce-scatter.25
  948.3 18.1 reduce-scatter.27
  1029.8 35.2 all-reduce.9
  1070.3 190.1 all-reduce.11
where the time goes:
time: 1280 us
  waiting for transfers between devices  923 us (72%)
  matrix products  128 us (10%)
  other arithmetic  83.2 us (6%)
  local copies, waits for them, and re-layouts  66.2 us (5%)
  blocking collectives  59.2 us (5%)
  between operations  16.5 us (1%)
    psum x1, waiting for transfers between devices, per_device(): lax.psum((grad_qkvw, grad_pair, grad_outw, grad_up, grad_upb, grad_down,...  194 us
    dot_general x38, matrix products, product(): jnp.einsum(einsum_form, left_op, right_op, preferred_element_type=jnp.flo...  125 us
    all_gather x2, waiting for transfers between devices, per_device(): forward_first_in = lax.all_gather(normed, 'tensor', axis=1, tiled=True)  98.2 us
    all_gather x2, waiting for transfers between devices, per_device(): lax.all_gather(grad_mid.astype(jnp.bfloat16), 'tensor', axis=1, tiled=True)  98 us
    all_gather x2, waiting for transfers between devices, per_device(): forward_second_in = lax.all_gather(second, 'tensor', axis=1, tiled=True)  95.8 us
    reduce_scatter x2, waiting for transfers between devices, per_device(): lax.psum_scatter(product('isc,cd->isd', forward_mixed_heads, out_weight[l...  92.9 us
    reduce_scatter x2, waiting for transfers between devices, per_device(): lax.psum_scatter(product('isf,fd->isd', forward_active, down_weight[layer...  88.5 us
    reduce_scatter x2, waiting for transfers between devices, per_device(): lax.psum_scatter(product('isf,df->isd', grad_hidden, up_weight[layer_idx]...  88.3 us
  transfers between devices with their start and end apart: 19, of which 18 were waited for; matrix products, arithmetic and copies ran while one was open for 8% of the time, Pallas kernels for 0%

commit v1 on v0

v1 whole, which is shorter than its diff:
```python
import jax
import jax.numpy as jnp
from jax import lax
from jax.sharding import PartitionSpec as P

HEAD_DIM = 64
LAYERS = 2
PROMPTS = 50
AXES = ("dp", "tensor")
epsilon = 1e-06
bf16 = jnp.bfloat16
f32 = jnp.float32


def dot(left, right, left_dim, right_dim):
    return lax.dot_general(
        left, right, (((left_dim,), (right_dim,)), ((), ())), preferred_element_type=f32
    )


def norm_parts(rows):
    centre = rows - jnp.mean(rows, axis=-1, keepdims=True)
    spread = jnp.mean(centre * centre, axis=-1, keepdims=True)
    scale = lax.rsqrt(spread + epsilon)
    return centre * scale, scale


def norm_back(hat, scale, gain, grad):
    inner = grad * gain
    along = jnp.mean(inner * hat, axis=-1, keepdims=True)
    return scale * (inner - jnp.mean(inner, axis=-1, keepdims=True) - hat * along)


def gate_pair(pre):
    half = 0.5 * (1.0 + lax.erf(pre * (0.5**0.5)))
    slope = half + pre * jnp.exp(-0.5 * pre * pre) * 0.3989422804014327
    return (pre * half).astype(bf16), slope.astype(bf16)


def reversed_bits(value, bits):
    return sum(((value >> b) & 1) << (bits - 1 - b) for b in range(bits))


def xor_order(arr, axis, index, bits):
    for b in range(bits):
        shape = arr.shape
        split = shape[:axis] + (shape[axis] >> (b + 1), 2, 1 << b) + shape[axis + 1 :]
        parts = arr.reshape(split)
        arr = jnp.where(((index >> b) & 1) == 1, jnp.flip(parts, axis + 1), parts).reshape(shape)
    return arr


def build(dp_size, tensor_size):
    planes = dp_size // 2
    bits = planes.bit_length() - 1
    zbits = tensor_size.bit_length() - 1

    def send(arr, target):
        pairs = []
        for dp in range(dp_size):
            for z in range(tensor_size):
                to = target(dp >> 1, dp & 1, z)
                if to is not None:
                    plane, core, depth = to
                    pairs.append((dp * tensor_size + z, (plane * 2 + core) * tensor_size + depth))
        return lax.ppermute(arr, AXES, pairs)

    def other_core(p, c, z):
        return p, 1 - c, z

    def along(k):
        return lambda p, c, z: (p, c, z ^ k)

    def flip(step, turned, only=None):
        def target(p, c, z):
            if only is not None and c != only:
                return None
            back = turned(c)
            return p ^ (1 << ((bits - 1 - step) if back else step)), c, z

        return target

    def plane_gather(piece, turned, only=None):
        acc = piece[None]
        for step in range(bits):
            got = send(acc, flip(step, turned, only))
            acc = jnp.concatenate([acc, got], axis=0)
        return acc

    def plane_scatter(acc, turned, extra=None):
        for step in range(bits):
            pairs = acc.reshape((acc.shape[0] // 2, 2) + acc.shape[1:])
            got = send(pairs[:, 1], flip(step, turned))
            acc = (pairs[:, 0].astype(f32) + got.astype(f32)).astype(bf16)
        return acc[0]

    def by_core(c):
        return c

    def per_device(
        tokens,
        cotangent,
        task_ids,
        key_mask,
        prompts,
        norm_gain,
        norm_bias,
        qkv_weight,
        qv_bias,
        out_weight,
        branch_bias,
        up_weight,
        up_bias,
        down_weight,
    ):
        group, rows_local, width = tokens.shape
        images = group // 2
        seq = rows_local * tensor_size
        heads = qkv_weight.shape[2] // (3 * HEAD_DIM)
        hidden = up_weight.shape[2]
        half_units = hidden // 2
        unit_q = half_units // planes
        dim_q = HEAD_DIM // planes
        task_count = prompts.shape[1]
        per_dev = task_count // dp_size
        score_scale = HEAD_DIM ** (-0.5)
        place = lax.axis_index("dp")
        z = lax.axis_index("tensor")
        core = place & 1
        plane = place >> 1
        plane_back = reversed_bits(plane, bits)
        first_core = core == 0
        odd = z & 1
        all_rows = images * seq

        def pick(arr, index, axis):
            return lax.dynamic_index_in_dim(arr, index, axis, keepdims=False)

        def ordered(arr, axis, index):
            parts = [pick(arr, index ^ r, axis) for r in range(planes)]
            return jnp.stack(parts, axis=0)

        def join(mine, theirs, axis):
            return jnp.where(
                first_core,
                jnp.concatenate([mine, theirs], axis),
                jnp.concatenate([theirs, mine], axis),
            )

        def gather_images(arr):
            one = lax.dynamic_slice_in_dim(arr, odd * images, images, 0)
            two = lax.dynamic_slice_in_dim(arr, (1 - odd) * images, images, 0)
            got_one = send(one, lambda p, c, d: (p, d >> 1, 2 * c + (d & 1)))
            got_two = send(two, lambda p, c, d: (p, d >> 1, 2 * c + 1 - (d & 1)))
            half = jnp.where(
                odd == 0,
                jnp.concatenate([got_one, got_two], 1),
                jnp.concatenate([got_two, got_one], 1),
            )
            return join(half, send(half, other_core), 1)

        def spread_images(arr):
            one = lax.dynamic_slice_in_dim(arr, rows_local * (2 * core + odd), rows_local, 1)
            two = lax.dynamic_slice_in_dim(arr, rows_local * (2 * core + 1 - odd), rows_local, 1)
            got_one = send(one, lambda p, c, d: (p, d >> 1, 2 * c + (d & 1)))
            got_two = send(two, lambda p, c, d: (p, d >> 1, 2 * c + 1 - (d & 1)))
            return jnp.where(
                odd == 0,
                jnp.concatenate([got_one, got_two], 0),
                jnp.concatenate([got_two, got_one], 0),
            )

        def exchange(part):
            part = part.astype(bf16)
            return part.astype(f32) + send(part, other_core).astype(f32)

        facts = jnp.concatenate([key_mask, task_ids], axis=1)
        facts = lax.dynamic_slice_in_dim(facts, odd * images, images, 0)
        facts = jnp.where(core == (z >> 1), facts, send(facts, other_core))
        mask, tasks = facts[:, :seq], facts[:, seq:]
        valid = (mask > 0)[:, None, None, :]
        row_mask = mask.astype(f32)[:, :, None]

        gains = norm_gain.astype(f32)
        shifts = norm_bias.astype(f32)
        biases = branch_bias.astype(f32)

        bias_pack = jnp.concatenate([up_bias, qv_bias], axis=1)
        bias_all = lax.all_gather(bias_pack, "tensor", axis=0)
        bias_all = xor_order(bias_all, 0, z, zbits).astype(f32)

        def turned_attn(layer):
            return lambda c: layer % 2

        def attn_place(layer):
            return plane_back if layer % 2 else plane

        unit_place = jnp.where(first_core, plane, plane_back)
        unit_place_other = jnp.where(first_core, plane_back, plane)

        def attn_weights(layer):
            qkv_rows = qkv_weight[layer].T.reshape(heads, 3, HEAD_DIM, width).swapaxes(0, 1)
            out_rows = out_weight[layer].reshape(1, heads, HEAD_DIM, width)
            own = jnp.concatenate([qkv_rows, out_rows], axis=0)
            own = own.reshape(4, heads, planes, dim_q, width)
            own = ordered(own, 2, attn_place(layer))
            piece = own[0]
            turned = turned_attn(layer)
            near = send(piece, lambda p, c, d: (p, c, d ^ (1 + c)))
            far = send(piece, lambda p, c, d: (p, c, d ^ 3) if c else None)
            near = plane_gather(near, turned)
            far = plane_gather(far, turned, only=1)
            whole = jnp.stack([jnp.where(first_core, own, far), near])
            whole = whole.transpose(2, 0, 3, 1, 4, 5)
            whole = whole.reshape(4, 2 * heads * HEAD_DIM, width)
            pair = bias_all[:, layer, hidden:].reshape(tensor_size, heads, 2, planes, dim_q)
            pair = xor_order(pair, 3, attn_place(layer), bits)
            pair = jnp.where(first_core, pair[:2], jnp.flip(pair[2:], 0))
            pair = pair.transpose(2, 0, 1, 3, 4).reshape(2, 2 * heads * HEAD_DIM)
            return whole[:3].reshape(-1, width), whole[3], pair[0], pair[1]

        def mlp_weights(layer):
            own = jnp.stack([up_weight[layer].T, down_weight[layer]])
            own = own.reshape(2, 2, planes, unit_q, width)
            own = ordered(pick(own, core, 1), 1, unit_place)
            piece = own[0]
            got = jnp.stack([send(piece, along(k)) for k in range(1, tensor_size)])
            got = plane_gather(got, by_core)
            whole = jnp.concatenate([own[:, None], got], axis=1)
            whole = whole.transpose(2, 0, 1, 3, 4).reshape(2, -1, width)
            bias = bias_all[:, layer, :hidden].reshape(tensor_size, 2, planes, unit_q)
            bias = xor_order(pick(bias, core, 1), 1, unit_place, bits)
            return whole[0], whole[1], bias.swapaxes(0, 1).reshape(-1)

        def heads_of(arr):
            return arr.reshape(images, seq, 2 * heads, HEAD_DIM)

        def scores_of(query, key):
            raw = jnp.einsum("iqhe,ikhe->ihqk", query, key, preferred_element_type=f32)
            return jnp.where(valid, raw, -1000000000.0)

        inner = 2 * heads * HEAD_DIM
        x = gather_images(tokens).astype(f32)
        kept = []
        for layer in range(LAYERS):
            chosen = jnp.stack(
                [pick(prompts[layer], tasks[i, layer], 0) for i in range(images)]
            ).astype(f32)
            xp = jnp.concatenate([x[:, :1], chosen, x[:, 1 + PROMPTS :]], axis=1)
            xp = xp.reshape(all_rows, width)
            hat, scale = norm_parts(xp)
            first_in = (hat * gains[layer, 0] + shifts[layer, 0]).astype(bf16)
            w_qkv, w_out, q_bias, v_bias = attn_weights(layer)
            qkv = dot(first_in, w_qkv, 1, 1)
            query = heads_of(((qkv[:, :inner] + q_bias) * score_scale).astype(bf16))
            key = heads_of(qkv[:, inner : 2 * inner].astype(bf16))
            value = heads_of((qkv[:, 2 * inner :] + v_bias).astype(bf16))
            scores = scores_of(query, key)
            peak = jnp.max(scores, axis=-1, keepdims=True)
            exps = jnp.exp(scores - peak)
            total = jnp.sum(exps, axis=-1, keepdims=True)
            probs = (exps / total).astype(bf16)
            log_total = peak + jnp.log(total)
            mixed = jnp.einsum("ihqk,ikhe->iqhe", probs, value, preferred_element_type=f32)
            mixed = mixed.astype(bf16).reshape(all_rows, inner)
            middle = xp + (exchange(dot(mixed, w_out, 1, 0)) + biases[layer, 0])
            hat_two, scale_two = norm_parts(middle)
            second_in = (hat_two * gains[layer, 1] + shifts[layer, 1]).astype(bf16)
            w_up, w_down, u_bias = mlp_weights(layer)
            active, slope = gate_pair(dot(second_in, w_up, 1, 1) + u_bias)
            result = middle + (exchange(dot(active, w_down, 1, 0)) + biases[layer, 1])
            x = result.reshape(images, seq, width)
            kept.append(
                (xp, middle, first_in, query, key, value, log_total, mixed, second_in, active, slope)
                + (w_qkv, w_out, w_up, w_down)
            )
        out = spread_images((x * row_mask).astype(bf16))

        grad_x = (gather_images(cotangent).astype(f32) * row_mask).reshape(all_rows, width)
        weight_grads = [None] * LAYERS
        small = [None] * LAYERS
        prompt_parts = [None] * LAYERS
        for layer in reversed(range(LAYERS)):
            (xp, middle, first_in, query, key, value, log_total, mixed, second_in, active, slope) = kept[
                layer
            ][:11]
            w_qkv, w_out, w_up, w_down = kept[layer][11:]
            bias_mlp = jnp.sum(grad_x, axis=0)
            down_in = grad_x.astype(bf16)
            grad_down = dot(active, down_in, 0, 0).astype(bf16)
            grad_hidden = (dot(down_in, w_down, 1, 1) * slope.astype(f32)).astype(bf16)
            grad_upb = jnp.sum(grad_hidden.astype(f32), axis=0)
            grad_up = dot(grad_hidden, second_in, 0, 0).astype(bf16)
            back = exchange(dot(grad_hidden, w_up, 1, 0))
            hat, scale = norm_parts(middle)
            grad_mid = grad_x + norm_back(hat, scale, gains[layer, 1], back)
            gain_two, shift_two = jnp.sum(back * hat, axis=0), jnp.sum(back, axis=0)
            bias_attn = jnp.sum(grad_mid, axis=0)
            attn_in = grad_mid.astype(bf16)
            grad_out = dot(mixed, attn_in, 0, 0).astype(bf16)
            grad_mixed = heads_of(dot(attn_in, w_out, 1, 1).astype(bf16))
            probs = jnp.exp(scores_of(query, key) - log_total)
            probs_low = probs.astype(bf16)
            grad_value = jnp.einsum(
                "ihqk,iqhe->ikhe", probs_low, grad_mixed, preferred_element_type=f32
            ).astype(bf16)
            grad_probs = jnp.einsum(
                "iqhe,ikhe->ihqk", grad_mixed, value, preferred_element_type=f32
            )
            grad_scores = (
                probs * (grad_probs - jnp.sum(probs * grad_probs, axis=-1, keepdims=True))
            ).astype(bf16)
            grad_query = jnp.einsum(
                "ihqk,ikhe->iqhe", grad_scores, key, preferred_element_type=f32
            ).astype(bf16) * bf16(score_scale)
            grad_key = jnp.einsum(
                "ihqk,iqhe->ikhe", grad_scores, query, preferred_element_type=f32
            ).astype(bf16)
            grad_qkv = jnp.concatenate(
                [g.reshape(all_rows, inner) for g in (grad_query, grad_key, grad_value)], axis=1
            )
            grad_qkvw = dot(grad_qkv, first_in, 0, 0).astype(bf16)
            grad_qb = jnp.sum(grad_qkv[:, :inner].astype(f32), axis=0)
            grad_vb = jnp.sum(grad_qkv[:, 2 * inner :].astype(f32), axis=0)
            back = exchange(dot(grad_qkv, w_qkv, 1, 0))
            hat, scale = norm_parts(xp)
            grad_in = grad_mid + norm_back(hat, scale, gains[layer, 0], back)
            gain_one, shift_one = jnp.sum(back * hat, axis=0), jnp.sum(back, axis=0)
            grad_in = grad_in.reshape(images, seq, width)
            at_prompts = grad_in[:, 1 : 1 + PROMPTS]
            grad_x = jnp.concatenate(
                [grad_in[:, :1], jnp.zeros_like(at_prompts), grad_in[:, 1 + PROMPTS :]], axis=1
            ).reshape(all_rows, width)

            units = jnp.stack([grad_up, grad_down]).reshape(2, planes, tensor_size, unit_q, width)
            units = plane_scatter(units.transpose(1, 2, 0, 3, 4), by_core)
            total = units[0].astype(f32)
            for k in range(1, tensor_size):
                total = total + send(units[k], along(k)).astype(f32)
            units = plane_gather(total.astype(bf16), by_core)
            units = xor_order(units, 0, unit_place, bits).swapaxes(0, 1)
            units = units.reshape(2, half_units, width)
            units = join(units, send(units, other_core), 1).astype(f32)
            full_up, full_down = units[0].T, units[1]

            turned = turned_attn(layer)
            parts = jnp.concatenate([grad_qkvw, grad_out], axis=0)
            parts = parts.reshape(4, 2, heads, planes, dim_q, width).transpose(3, 1, 0, 2, 4, 5)
            parts = plane_scatter(parts, turned)
            near = send(parts[1], lambda p, c, d: (p, c, d ^ (1 + c)))
            far = send(parts[0], lambda p, c, d: (p, c, d ^ 3) if c else None)
            total = jnp.where(first_core, parts[0], far).astype(f32) + near.astype(f32)
            total = total.astype(bf16)
            theirs = jnp.where(first_core, total[2:], total[:2])
            mine = jnp.where(first_core, total[:2], total[2:])
            mine = (mine.astype(f32) + send(theirs, other_core).astype(f32)).astype(bf16)
            parts = plane_gather(mine, turned)
            parts = xor_order(parts, 0, attn_place(layer), bits).transpose(1, 2, 0, 3, 4)
            parts = parts.reshape(2, heads, HEAD_DIM, width)
            parts = join(parts, send(parts, other_core), 0).astype(f32)
            full_qkv = parts[:3].swapaxes(0, 1).reshape(heads * 3 * HEAD_DIM, width).T
            full_out = parts[3].reshape(heads * HEAD_DIM, width)
            weight_grads[layer] = (full_qkv, full_out, full_up, full_down)

            norms = jnp.stack([gain_one, gain_two, shift_one, shift_two, bias_attn, bias_mlp])
            norms = 0.5 * norms.reshape(6, tensor_size, width // tensor_size)
            upb = grad_upb.reshape(planes, tensor_size, unit_q)
            upb = xor_order(xor_order(upb, 0, unit_place, bits), 1, z, zbits).swapaxes(0, 1)
            upb = upb.reshape(tensor_size, half_units)
            upb = join(upb, jnp.zeros_like(upb), 1)
            pair = jnp.stack([grad_qb, grad_vb]).reshape(2, 2, heads, planes, dim_q)
            pair = xor_order(pair, 3, attn_place(layer), bits).transpose(1, 2, 0, 3, 4)
            pair = pair.reshape(2, heads * 2 * HEAD_DIM)
            pair = join(pair, jnp.zeros_like(pair), 0)
            pair = jnp.where(
                first_core, pair, jnp.concatenate([pair[:2], jnp.flip(pair[2:], 0)], axis=0)
            )
            pair = xor_order(pair, 0, z, zbits)
            block = width // tensor_size
            small[layer] = jnp.concatenate(
                [
                    norms,
                    upb.reshape(tensor_size, -1, block).swapaxes(0, 1),
                    pair.reshape(tensor_size, -1, block).swapaxes(0, 1),
                ],
                axis=0,
            )
            owner = (plane ^ jnp.arange(planes)) * 2 + core
            task_list = owner[:, None] * per_dev + jnp.arange(per_dev)[None, :]
            hot = (task_list[:, :, None] == tasks[None, None, :, layer]).astype(f32)
            picked = sum(
                hot[:, :, i, None, None] * at_prompts[i][None, None] for i in range(images)
            )
            prompt_parts[layer] = picked.reshape(planes, per_dev * PROMPTS, tensor_size, block)

        grad_tokens = spread_images(grad_x.reshape(images, seq, width).astype(bf16))

        small_all = jnp.concatenate(small, axis=0)
        small_rows = small_all.shape[0]
        small_all = exchange(small_all)
        wanted = jnp.concatenate(prompt_parts, axis=1).astype(bf16)
        for step in range(bits):
            pairs = wanted.reshape((wanted.shape[0] // 2, 2) + wanted.shape[1:])
            flat = pairs[:, 1].reshape(-1, tensor_size, block)
            got = send(
                jnp.concatenate([flat, small_all.astype(bf16)], axis=0), flip(step, lambda c: 0)
            )
            small_all = small_all.astype(bf16).astype(f32) + got[-small_rows:].astype(f32)
            wanted = (
                pairs[:, 0].astype(f32) + got[:-small_rows].reshape(pairs[:, 0].shape).astype(f32)
            ).astype(bf16)
        tail = jnp.concatenate([wanted[0].astype(f32), small_all], axis=0)
        tail = xor_order(tail, 1, z, zbits)
        for step in reversed(range(zbits)):
            size = 1 << step
            got = send(tail[:, size:].astype(bf16), along(size))
            tail = tail[:, :size] + got.astype(f32)
        tail = tail[:, 0]
        prompt_rows = LAYERS * per_dev * PROMPTS
        grad_prompts = tail[:prompt_rows].reshape(LAYERS, per_dev, PROMPTS, block)
        sums = tail[prompt_rows:].reshape(LAYERS, -1, block)
        up_rows = hidden // block
        grad_upb = sums[:, 6 : 6 + up_rows].reshape(LAYERS, hidden)
        grad_pair = sums[:, 6 + up_rows :].reshape(LAYERS, heads * 2 * HEAD_DIM)
        full_qkv, full_out, full_up, full_down = (
            jnp.stack(both) for both in zip(*weight_grads)
        )
        return (
            out,
            grad_tokens,
            grad_prompts,
            sums[:, 0:2],
            sums[:, 2:4],
            full_qkv,
            grad_pair,
            full_out,
            sums[:, 4:6],
            full_up,
            grad_upb,
            full_down,
        )

    return per_device


def solution(mesh):
    placed = (
        P("dp", "tensor", None),
        P("dp", "tensor", None),
        P("dp", None),
        P("dp", None),
        P(),
        P(),
        P(),
        P(None, None, "tensor"),
        P(None, "tensor"),
        P(None, "tensor", None),
        P(),
        P(None, None, "tensor"),
        P(None, "tensor"),
        P(None, "tensor", None),
    )
    return jax.shard_map(
        build(mesh.shape["dp"], mesh.shape["tensor"]),
        mesh=mesh,
        in_specs=placed,
        out_specs=(
            P("dp", "tensor", None),
            P("dp", "tensor", None),
            P(None, "dp", None, "tensor"),
            P(None, None, "tensor"),
            P(None, None, "tensor"),
            P(None, None, "tensor"),
            P(None, "tensor"),
            P(None, "tensor", None),
            P(None, None, "tensor"),
            P(None, None, "tensor"),
            P(None, "tensor"),
            P(None, "tensor", None),
        ),
        check_vma=False,
    )
```

time: 1280 us -> 705 us (0.55)
  waiting for transfers between devices: 923 us -> 152 us
  local copies, waits for them, and re-layouts: 66.2 us -> 169 us
  starting transfers between devices: 2.16 us -> 101 us
  other arithmetic: 83.2 us -> 143 us
  blocking collectives: 59.2 us -> 22.2 us
  matrix products: 128 us -> 93 us
    all_gather x8 -> x0, waiting for transfers between devices: 374 us -> none  [the longest x2 98.2 us: per_device(): forward_first_in = lax.all_gather(normed, 'tensor', axis=1, tiled=True)]
    reduce_scatter x8 -> x0, waiting for transfers between devices: 317 us -> none  [the longest x2 92.9 us: per_device(): lax.psum_scatter(product('isc,cd->isd', forward_mixed_heads, out_weight[l...]
    psum x1 -> x0, waiting for transfers between devices: 194 us -> none  [per_device(): lax.psum((grad_qkvw, grad_pair, grad_outw, grad_up, grad_upb, grad_down,...]
    ppermute x0 -> x78, waiting for transfers between devices: none -> 152 us  [send(): return lax.ppermute(arr, AXES, pairs)]
    ppermute x0 -> x78, starting transfers between devices: none -> 101 us  [send(): return lax.ppermute(arr, AXES, pairs)]
    unnamed x1 -> x0, blocking collectives: 59.2 us -> none
    reshape x0 -> x29, local copies, waits for them, and re-layouts: none -> 44.3 us  [the longest x16 41.1 us: heads_of(): return arr.reshape(images, seq, 2 * heads, HEAD_DIM)]
    unnamed x21 -> x0, waiting for transfers between devices: 38.9 us -> none
  transfers between devices with their start and end apart: 19 -> 78, of which waited for: 18 -> 15; matrix products, arithmetic and copies ran while one was open for 8% -> 50% of each run, Pallas kernels for 0% -> 0%
where the time goes in v1:
time: 705 us; the launch traced here: 696 us
  local copies, waits for them, and re-layouts  169 us (24%)
  waiting for transfers between devices  152 us (22%)
  other arithmetic  143 us (20%)
  starting transfers between devices  101 us (14%)
  matrix products  93 us (13%)
  blocking collectives  22.2 us (3%)
  between operations  16.4 us (2%)
    ppermute x78, waiting for transfers between devices, send(): return lax.ppermute(arr, AXES, pairs)  152 us
    ppermute x78, starting transfers between devices, send(): return lax.ppermute(arr, AXES, pairs)  101 us
    dot_general x24, matrix products, dot(): lax.dot_general(left, right, (((left_dim,), (right_dim,)), ((), ())), pre...  65.6 us
    reshape x16, local copies, waits for them, and re-layouts, heads_of(): return arr.reshape(images, seq, 2 * heads, HEAD_DIM)  41.1 us
    unnamed x442, local copies, waits for them, and re-layouts  36.9 us
    all_gather x1, blocking collectives, per_device(): bias_all = lax.all_gather(bias_pack, 'tensor', axis=0)  22.2 us
    concatenate x14, other arithmetic, plane_gather(): acc = jnp.concatenate([acc, got], axis=0)  16.9 us
  transfers between devices with their start and end apart: 78, of which 15 were waited for; matrix products, arithmetic and copies ran while one was open for 50% of the time, Pallas kernels for 0%

profile of v1, /device:TPU:0, one launch (start us, length us, event | category | flops | bytes accessed | tf_op | source)
XLA Modules:
  0.0 696.1 jit_solution(4958574097390096396)
XLA Ops:
  10.4 3.7 collective-permute-start
  16.9 22.2 %all-gather.1 = bf16[4,2,1152]{2,1,0:T(2,128)(2,1)S(1)} all-gather(bf16[1,2,1152]{2,1,0:T(2,128)(2,1)S(1)} %maximum_bitcast_fusion.10), channel_id=2, replica_groups=mesh['dp'=8,'tensor'=4] {'tensor'}, dimensions={0}, use_global_device_ids=true | all-gather | bytes 23040 | tf_op jit(solution)/shard_map/all_gather | solution.py:189
  74.3 4.1 collective-permute-start.13
  92.6 10.3 %collective-permute-done.12 = bf16[2,96,768]{2,1,0:T(8,128)(2,1)S(1)} collective-permute-done((bf16[2,96,768]{2,1,0:T(8,128)(2,1)S(1)}, bf16[2,96,768]{2,1,0:T(8,128)(2,1)S(1)}, u32[]{:S(2)}, u32[]{:S(2)}) %collective-permute-start.12) | collective-permute-done | bytes 294944 | tf_op jit(solution)/shard_map/ppermute | solution.py:66
  113.9 10.9 %collective-permute-done.9 = bf16[2,4,3,16,768]{4,3,0,2,1:T(8,128)(2,1)S(1)} collective-permute-done((bf16[2,4,3,16,768]{4,3,0,2,1:T(8,128)(2,1)S(1)}, bf16[2,4,3,16,768]{4,3,0,2,1:T(8,128)(2,1)S(1)}, u32[]{:S(2)}, u32[]{:S(2)}) %collective-permute-start.9) | collective-permute-done | bytes 589856 | tf_op jit(solution)/shard_map/ppermute | solution.py:66
  191.1 27.1 %collective-permute-done.21 = bf16[1,4,3,16,768]{4,3,2,1,0:T(8,128)(2,1)S(1)} collective-permute-done((bf16[1,4,3,16,768]{4,3,2,1,0:T(8,128)(2,1)}, bf16[1,4,3,16,768]{4,3,2,1,0:T(8,128)(2,1)S(1)}, u32[]{:S(2)}, u32[]{:S(2)}) %collective-permute-start.21) | collective-permute-done | bytes 294944 | tf_op jit(solution)/shard_map/ppermute | solution.py:66
  231.2 5.3 multiply_convert_fusion.5
  273.6 4.3 select_reduce_fusion
  306.4 4.5 convert_reduce_fusion
  317.6 5.4 convolution_convert_fusion
  323.6 4.7 convolution_convert_fusion.1
  333.1 3.5 multiply_reduce_fusion.2
  336.6 6.8 fusion.155
  350.1 4.2 multiply_reduce_fusion.1
  366.9 7.4 %collective-permute-start.36 = (bf16[768,768]{1,0:T(8,128)(2,1)}, bf16[768,768]{1,0:T(8,128)(2,1)}, u32[]{:S(2)}, u32[]{:S(2)}) collective-permute-start(bf16[768,768]{1,0:T(8,128)(2,1)} %convolution_convert_fusion.7), channel_id=1, source_target_pairs={{0,4},{1,5},{2,6},{3,7},{4,0},{5,1},{6,2},{7,3},{8,12},{9,13},{10,... | collective-permute-start | bytes 3538952 | tf_op jit(solution)/shard_map/ppermute | solution.py:66
  386.5 3.8 add_convert_fusion
  392.4 4.5 convert_reduce_fusion.1
  439.7 4.2 multiply_reduce_fusion
  468.1 3.7 collective-permute-done.55
  474.5 21.8 %collective-permute-done.73 = bf16[2,96,768]{2,1,0:T(8,128)(2,1)S(1)} collective-permute-done((bf16[2,96,768]{2,1,0:T(8,128)(2,1)S(1)}, bf16[2,96,768]{2,1,0:T(8,128)(2,1)S(1)}, u32[]{:S(2)}, u32[]{:S(2)}) %collective-permute-start.73) | collective-permute-done | bytes 294944 | tf_op jit(solution)/shard_map/ppermute | solution.py:66
  520.4 11.4 %collective-permute-start.40 = (bf16[3,64,768]{2,1,0:T(8,128)(2,1)}, bf16[3,64,768]{2,1,0:T(8,128)(2,1)}, u32[]{:S(2)}, u32[]{:S(2)}) collective-permute-start(bf16[3,64,768]{2,1,0:T(8,128)(2,1)} %get-tuple-element.214), channel_id=1, source_target_pairs={{0,1},{1,0},{2,5},{3,4},{4,3},{5,2},{6,7},{7,6},{8,9},{9,8},{10,13... | collective-permute-start | bytes 884744 | tf_op jit(solution)/shard_map/ppermute | solution.py:66
  531.8 3.9 collective-permute-start.39
  557.6 30.2 %collective-permute-done.42 = bf16[224,4,192]{2,1,0:T(4,128)(2,1)S(1)} collective-permute-done((bf16[224,4,192]{2,1,0:T(4,128)(2,1)S(1)}, bf16[224,4,192]{2,1,0:T(4,128)(2,1)S(1)}, u32[]{:S(2)}, u32[]{:S(2)}) %collective-permute-start.42) | collective-permute-done | bytes 344096 | tf_op jit(solution)/shard_map/ppermute | solution.py:66
  602.2 12.9 %collective-permute-done.63 = bf16[1,4,2,96,768]{4,3,1,2,0:T(8,128)(2,1)} collective-permute-done((bf16[1,4,2,96,768]{4,3,1,2,0:T(8,128)(2,1)}, bf16[1,4,2,96,768]{4,3,1,2,0:T(8,128)(2,1)}, u32[]{:S(2)}, u32[]{:S(2)}) %collective-permute-start.63) | collective-permute-done | bytes 1179680 | tf_op jit(solution)/shard_map/ppermute | solution.py:66
  621.3 4.2 collective-permute-done.66
  625.6 10.1 %collective-permute-done.65 = bf16[2,96,768]{2,1,0:T(8,128)(2,1)S(1)} collective-permute-done((bf16[2,96,768]{2,1,0:T(8,128)(2,1)S(1)}, bf16[2,96,768]{2,1,0:T(8,128)(2,1)S(1)}, u32[]{:S(2)}, u32[]{:S(2)}) %collective-permute-start.65) | collective-permute-done | bytes 294944 | tf_op jit(solution)/shard_map/ppermute | solution.py:66
  635.8 5.3 collective-permute-start.67
  641.4 4.1 collective-permute-done.44
  646.6 4.5 collective-permute-done.49
  664.2 5.8 collective-permute-done.52
  685.7 6.0 copy.812
  691.7 4.2 pad_maximum_fusion.3
  (987 shorter events, 414.5 us)
Async XLA Ops:
  5.1 83.7 %collective-permute-start.7 = (bf16[4,3,16,768]{3,2,1,0:T(8,128)(2,1)}, bf16[4,3,16,768]{3,2,1,0:T(8,128)(2,1)}, u32[]{:S(2)}, u32[]{:S(2)}) collective-permute-start(bf16[4,3,16,768]{3,2,1,0:T(8,128)(2,1)} %bitcast.18), channel_id=1, source_target_pairs={{0,1},{1,0},{2,3},{3,2},{4,6},{5,7},{6,4},{7,5},{8,9},{9,8},{10,11... | collective-permute-start | bytes 884744 | tf_op jit(solution)/shard_map/ppermute | solution.py:66
  8.2 81.5 %collective-permute-start.4 = (bf16[4,3,16,768]{3,2,1,0:T(8,128)(2,1)}, bf16[4,3,16,768]{3,2,1,0:T(8,128)(2,1)}, u32[]{:S(2)}, u32[]{:S(2)}) collective-permute-start(bf16[4,3,16,768]{3,2,1,0:T(8,128)(2,1)} %bitcast.18), channel_id=1, source_target_pairs={{4,7},{5,6},{6,5},{7,4},{12,15},{13,14},{14,13},{15,12},{20,23},{2... | collective-permute-start | bytes 884744 | tf_op jit(solution)/shard_map/ppermute | solution.py:66
  10.4 76.4 %collective-permute-start.1 = (bf16[3,64,768]{2,1,0:T(8,128)(2,1)}, bf16[3,64,768]{2,1,0:T(8,128)(2,1)}, u32[]{:S(2)}, u32[]{:S(2)}) collective-permute-start(bf16[3,64,768]{2,1,0:T(8,128)(2,1)} %get-tuple-element.240), channel_id=1, source_target_pairs={{0,1},{1,0},{2,5},{3,4},{4,3},{5,2},{6,7},{7,6},{8,9},{9,8},{10,13... | collective-permute-start | bytes 884744 | tf_op jit(solution)/shard_map/ppermute | solution.py:66
  10.4 76.5 %collective-permute-start = (bf16[3,64,768]{2,1,0:T(8,128)(2,1)}, bf16[3,64,768]{2,1,0:T(8,128)(2,1)}, u32[]{:S(2)}, u32[]{:S(2)}) collective-permute-start(bf16[3,64,768]{2,1,0:T(8,128)(2,1)} %get-tuple-element.239), channel_id=1, source_target_pairs={{0,0},{1,1},{2,4},{3,5},{4,2},{5,3},{6,6},{7,7},{8,8},{9,9},{10,12... | collective-permute-start | bytes 884744 | tf_op jit(solution)/shard_map/ppermute | solution.py:66
  14.8 59.5 %collective-permute-start.3 = (s32[3,258]{1,0:T(4,128)}, s32[3,258]{1,0:T(4,128)}, u32[]{:S(2)}, u32[]{:S(2)}) collective-permute-start(s32[3,258]{1,0:T(4,128)} %fusion.147), channel_id=1, source_target_pairs={{0,4},{1,5},{2,6},{3,7},{4,0},{5,1},{6,2},{7,3},{8,12},{9,13},{10,... | collective-permute-start | bytes 9296 | tf_op jit(solution)/shard_map/ppermute | solution.py:66
  102.9 56.1 %collective-permute-start.26 = (bf16[2,96,768]{2,1,0:T(8,128)(2,1)}, bf16[2,96,768]{2,1,0:T(8,128)(2,1)}, u32[]{:S(2)}, u32[]{:S(2)}) collective-permute-start(bf16[2,96,768]{2,1,0:T(8,128)(2,1)} %bitcast.104), channel_id=1, source_target_pairs={{0,3},{1,2},{2,1},{3,0},{4,7},{5,6},{6,5},{7,4},{8,11},{9,10},{10,... | collective-permute-start | bytes 884744 | tf_op jit(solution)/shard_map/ppermute | solution.py:66
  105.5 62.1 %collective-permute-start.25 = (bf16[2,96,768]{2,1,0:T(8,128)(2,1)}, bf16[2,96,768]{2,1,0:T(8,128)(2,1)}, u32[]{:S(2)}, u32[]{:S(2)}) collective-permute-start(bf16[2,96,768]{2,1,0:T(8,128)(2,1)} %bitcast.104), channel_id=1, source_target_pairs={{0,2},{1,3},{2,0},{3,1},{4,6},{5,7},{6,4},{7,5},{8,10},{9,11},{10,... | collective-permute-start | bytes 884744 | tf_op jit(solution)/shard_map/ppermute | solution.py:66
  105.7 69.0 %collective-permute-start.24 = (bf16[2,96,768]{2,1,0:T(8,128)(2,1)}, bf16[2,96,768]{2,1,0:T(8,128)(2,1)}, u32[]{:S(2)}, u32[]{:S(2)}) collective-permute-start(bf16[2,96,768]{2,1,0:T(8,128)(2,1)} %bitcast.104), channel_id=1, source_target_pairs={{0,1},{1,0},{2,3},{3,2},{4,5},{5,4},{6,7},{7,6},{8,9},{9,8},{10,11... | collective-permute-start | bytes 884744 | tf_op jit(solution)/shard_map/ppermute | solution.py:66
  124.8 51.6 %collective-permute-start.20 = (bf16[4,3,16,768]{3,2,1,0:T(8,128)(2,1)S(1)}, bf16[4,3,16,768]{3,2,1,0:T(8,128)(2,1)}, u32[]{:S(2)}, u32[]{:S(2)}) collective-permute-start(bf16[4,3,16,768]{3,2,1,0:T(8,128)(2,1)S(1)} %bitcast.710), channel_id=1, source_target_pairs={{0,1},{1,0},{2,3},{3,2},{4,6},{5,7},{6,4},{7,5},{8,9},{9,8},{10,11... | collective-permute-start | bytes 884744 | tf_op jit(solution)/shard_map/ppermute | solution.py:66
  126.2 44.4 %collective-permute-start.14 = (bf16[1,3,2,96,768]{4,3,2,1,0:T(8,128)(2,1)S(1)}, bf16[1,3,2,96,768]{4,3,2,1,0:T(8,128)(2,1)}, u32[]{:S(2)}, u32[]{:S(2)}) collective-permute-start(bf16[1,3,2,96,768]{4,3,2,1,0:T(8,128)(2,1)S(1)} %maximum_bitcast_fusion.8), channel_id=1, source_target_pairs={{0,8},{1,9},{2,10},{3,11},{4,20},{5,21},{6,22},{7,23},{8,0},{9,1},... | collective-permute-start | bytes 2654216 | tf_op jit(solution)/shard_map/ppermute | solution.py:66
  159.0 63.5 %collective-permute-start.10 = (bf16[768,768]{1,0:T(8,128)(2,1)}, bf16[768,768]{1,0:T(8,128)(2,1)}, u32[]{:S(2)}, u32[]{:S(2)}) collective-permute-start(bf16[768,768]{1,0:T(8,128)(2,1)} %convolution_convert_fusion.9), channel_id=1, source_target_pairs={{0,4},{1,5},{2,6},{3,7},{4,0},{5,1},{6,2},{7,3},{8,12},{9,13},{10,... | collective-permute-start | bytes 3538952 | tf_op jit(solution)/shard_map/ppermute | solution.py:66
  176.5 50.1 %collective-permute-start.15 = (bf16[2,3,2,96,768]{4,3,2,1,0:T(8,128)(2,1)}, bf16[2,3,2,96,768]{4,3,2,1,0:T(8,128)(2,1)}, u32[]{:S(2)}, u32[]{:S(2)}) collective-permute-start(bf16[2,3,2,96,768]{4,3,2,1,0:T(8,128)(2,1)} %pad_maximum_fusion.10), channel_id=1, source_target_pairs={{0,16},{1,17},{2,18},{3,19},{4,12},{5,13},{6,14},{7,15},{8,24},{9,... | collective-permute-start | bytes 5308424 | tf_op jit(solution)/shard_map/ppermute | solution.py:66
  178.6 39.6 %collective-permute-start.21 = (bf16[1,4,3,16,768]{4,3,2,1,0:T(8,128)(2,1)}, bf16[1,4,3,16,768]{4,3,2,1,0:T(8,128)(2,1)S(1)}, u32[]{:S(2)}, u32[]{:S(2)}) collective-permute-start(bf16[1,4,3,16,768]{4,3,2,1,0:T(8,128)(2,1)} %bitcast.84), channel_id=1, source_target_pairs={{0,16},{1,17},{2,18},{3,19},{4,20},{5,21},{6,22},{7,23},{8,24},{9,... | collective-permute-start | bytes 884744 | tf_op jit(solution)/shard_map/ppermute | solution.py:66
  184.5 35.5 %collective-permute-start.18 = (bf16[1,4,3,16,768]{4,3,2,1,0:T(8,128)(2,1)}, bf16[1,4,3,16,768]{4,3,2,1,0:T(8,128)(2,1)S(1)}, u32[]{:S(2)}, u32[]{:S(2)}) collective-permute-start(bf16[1,4,3,16,768]{4,3,2,1,0:T(8,128)(2,1)} %bitcast.714), channel_id=1, source_target_pairs={{4,20},{5,21},{6,22},{7,23},{12,28},{13,29},{14,30},{15,31},{20,4}... | collective-permute-start | bytes 884744 | tf_op jit(solution)/shard_map/ppermute | solution.py:66
  188.2 62.5 %collective-permute-start.27 = (bf16[1,3,2,96,768]{4,3,2,1,0:T(8,128)(2,1)}, bf16[1,3,2,96,768]{4,3,2,1,0:T(8,128)(2,1)}, u32[]{:S(2)}, u32[]{:S(2)}) collective-permute-start(bf16[1,3,2,96,768]{4,3,2,1,0:T(8,128)(2,1)} %maximum_bitcast_fusion.9), channel_id=1, source_target_pairs={{0,8},{1,9},{2,10},{3,11},{4,20},{5,21},{6,22},{7,23},{8,0},{9,1},... | collective-permute-start | bytes 2654216 | tf_op jit(solution)/shard_map/ppermute | solution.py:66
  253.7 39.5 %collective-permute-start.28 = (bf16[2,3,2,96,768]{4,3,2,1,0:T(8,128)(2,1)}, bf16[2,3,2,96,768]{4,3,2,1,0:T(8,128)(2,1)}, u32[]{:S(2)}, u32[]{:S(2)}) collective-permute-start(bf16[2,3,2,96,768]{4,3,2,1,0:T(8,128)(2,1)} %pad_maximum_fusion.11), channel_id=1, source_target_pairs={{0,16},{1,17},{2,18},{3,19},{4,12},{5,13},{6,14},{7,15},{8,24},{9,... | collective-permute-start | bytes 5308424 | tf_op jit(solution)/shard_map/ppermute | solution.py:66
  332.0 85.9 %collective-permute-start.70 = (bf16[2,4,2,96,768]{4,3,1,0,2:T(8,128)(2,1)}, bf16[2,4,2,96,768]{4,3,1,0,2:T(8,128)(2,1)}, u32[]{:S(2)}, u32[]{:S(2)}) collective-permute-start(bf16[2,4,2,96,768]{4,3,1,0,2:T(8,128)(2,1)} %slice_bitcast_fusion.1), channel_id=1, source_target_pairs={{0,8},{1,9},{2,10},{3,11},{4,20},{5,21},{6,22},{7,23},{8,0},{9,1},... | collective-permute-start | bytes 7077896 | tf_op jit(solution)/shard_map/ppermute | solution.py:66
  399.0 30.6 %collective-permute-start.37 = (bf16[768,768]{1,0:T(8,128)(2,1)S(1)}, bf16[768,768]{1,0:T(8,128)(2,1)}, u32[]{:S(2)}, u32[]{:S(2)}) collective-permute-start(bf16[768,768]{1,0:T(8,128)(2,1)S(1)} %convolution_convert_fusion.10), channel_id=1, source_target_pairs={{0,4},{1,5},{2,6},{3,7},{4,0},{5,1},{6,2},{7,3},{8,12},{9,13},{10,... | collective-permute-start | bytes 3538952 | tf_op jit(solution)/shard_map/ppermute | solution.py:66
  412.0 42.3 %collective-permute-start.54 = (bf16[2,2,4,3,16,768]{5,4,3,2,1,0:T(8,128)(2,1)}, bf16[2,2,4,3,16,768]{5,4,3,2,1,0:T(8,128)(2,1)}, u32[]{:S(2)}, u32[]{:S(2)}) collective-permute-start(bf16[2,2,4,3,16,768]{5,4,3,2,1,0:T(8,128)(2,1)} %bitcast.603), channel_id=1, source_target_pairs={{0,16},{1,17},{2,18},{3,19},{4,20},{5,21},{6,22},{7,23},{8,24},{9,... | collective-permute-start | bytes 3538952 | tf_op jit(solution)/shard_map/ppermute | solution.py:66
  421.5 37.1 %collective-permute-start.71 = (bf16[1,4,2,96,768]{4,3,1,2,0:T(8,128)(2,1)}, bf16[1,4,2,96,768]{4,3,1,2,0:T(8,128)(2,1)}, u32[]{:S(2)}, u32[]{:S(2)}) collective-permute-start(bf16[1,4,2,96,768]{4,3,1,2,0:T(8,128)(2,1)} %slice_bitcast_fusion.8), channel_id=1, source_target_pairs={{0,16},{1,17},{2,18},{3,19},{4,12},{5,13},{6,14},{7,15},{8,24},{9,... | collective-permute-start | bytes 3538952 | tf_op jit(solution)/shard_map/ppermute | solution.py:66
  462.5 33.8 %collective-permute-start.73 = (bf16[2,96,768]{2,1,0:T(8,128)(2,1)S(1)}, bf16[2,96,768]{2,1,0:T(8,128)(2,1)S(1)}, u32[]{:S(2)}, u32[]{:S(2)}) collective-permute-start(bf16[2,96,768]{2,1,0:T(8,128)(2,1)S(1)} %get-tuple-element.212), channel_id=1, source_target_pairs={{0,2},{1,3},{2,0},{3,1},{4,6},{5,7},{6,4},{7,5},{8,10},{9,11},{10,... | collective-permute-start | bytes 884744 | tf_op jit(solution)/shard_map/ppermute | solution.py:66
  463.3 32.9 %collective-permute-start.72 = (bf16[2,96,768]{2,1,0:T(8,128)(2,1)S(1)}, bf16[2,96,768]{2,1,0:T(8,128)(2,1)S(1)}, u32[]{:S(2)}, u32[]{:S(2)}) collective-permute-start(bf16[2,96,768]{2,1,0:T(8,128)(2,1)S(1)} %get-tuple-element.210), channel_id=1, source_target_pairs={{0,1},{1,0},{2,3},{3,2},{4,5},{5,4},{6,7},{7,6},{8,9},{9,8},{10,11... | collective-permute-start | bytes 884744 | tf_op jit(solution)/shard_map/ppermute | solution.py:66
  473.9 75.8 %collective-permute-start.62 = (bf16[2,4,2,96,768]{4,3,1,0,2:T(8,128)(2,1)}, bf16[2,4,2,96,768]{4,3,1,0,2:T(8,128)(2,1)}, u32[]{:S(2)}, u32[]{:S(2)}) collective-permute-start(bf16[2,4,2,96,768]{4,3,1,0,2:T(8,128)(2,1)} %slice_bitcast_fusion.4), channel_id=1, source_target_pairs={{0,8},{1,9},{2,10},{3,11},{4,20},{5,21},{6,22},{7,23},{8,0},{9,1},... | collective-permute-start | bytes 7077896 | tf_op jit(solution)/shard_map/ppermute | solution.py:66
  508.2 32.9 %collective-permute-start.76 = (bf16[2,2,96,768]{3,2,1,0:T(8,128)(2,1)}, bf16[2,2,96,768]{3,2,1,0:T(8,128)(2,1)}, u32[]{:S(2)}, u32[]{:S(2)}) collective-permute-start(bf16[2,2,96,768]{3,2,1,0:T(8,128)(2,1)} %pad_maximum_fusion.23), channel_id=1, source_target_pairs={{0,16},{1,17},{2,18},{3,19},{4,12},{5,13},{6,14},{7,15},{8,24},{9,... | collective-permute-start | bytes 1769480 | tf_op jit(solution)/shard_map/ppermute | solution.py:66
  510.9 29.2 %collective-permute-start.59 = (bf16[1,2,3,16,768]{4,3,2,1,0:T(8,128)(2,1)}, bf16[1,2,3,16,768]{4,3,2,1,0:T(8,128)(2,1)}, u32[]{:S(2)}, u32[]{:S(2)}) collective-permute-start(bf16[1,2,3,16,768]{4,3,2,1,0:T(8,128)(2,1)} %fusion.139), channel_id=1, source_target_pairs={{0,16},{1,17},{2,18},{3,19},{4,20},{5,21},{6,22},{7,23},{8,24},{9,... | collective-permute-start | bytes 442376 | tf_op jit(solution)/shard_map/ppermute | solution.py:66
  520.4 69.3 %collective-permute-start.40 = (bf16[3,64,768]{2,1,0:T(8,128)(2,1)}, bf16[3,64,768]{2,1,0:T(8,128)(2,1)}, u32[]{:S(2)}, u32[]{:S(2)}) collective-permute-start(bf16[3,64,768]{2,1,0:T(8,128)(2,1)} %get-tuple-element.214), channel_id=1, source_target_pairs={{0,1},{1,0},{2,5},{3,4},{4,3},{5,2},{6,7},{7,6},{8,9},{9,8},{10,13... | collective-permute-start | bytes 884744 | tf_op jit(solution)/shard_map/ppermute | solution.py:66
  531.8 59.1 %collective-permute-start.39 = (bf16[3,64,768]{2,1,0:T(8,128)(2,1)}, bf16[3,64,768]{2,1,0:T(8,128)(2,1)}, u32[]{:S(2)}, u32[]{:S(2)}) collective-permute-start(bf16[3,64,768]{2,1,0:T(8,128)(2,1)} %get-tuple-element.213), channel_id=1, source_target_pairs={{0,0},{1,1},{2,4},{3,5},{4,2},{5,3},{6,6},{7,7},{8,8},{9,9},{10,12... | collective-permute-start | bytes 884744 | tf_op jit(solution)/shard_map/ppermute | solution.py:66
  549.7 49.6 %collective-permute-start.46 = (bf16[2,2,4,3,16,768]{5,4,0,3,1,2:T(8,128)(2,1)}, bf16[2,2,4,3,16,768]{5,4,0,3,1,2:T(8,128)(2,1)}, u32[]{:S(2)}, u32[]{:S(2)}) collective-permute-start(bf16[2,2,4,3,16,768]{5,4,0,3,1,2:T(8,128)(2,1)} %slice_bitcast_fusion.12), channel_id=1, source_target_pairs={{0,8},{1,9},{2,10},{3,11},{4,12},{5,13},{6,14},{7,15},{8,0},{9,1},... | collective-permute-start | bytes 3538952 | tf_op jit(solution)/shard_map/ppermute | solution.py:66
  553.7 124.9 %collective-permute-start.77 = (bf16[2,384,768]{2,1,0:T(8,128)(2,1)S(1)}, bf16[2,384,768]{2,1,0:T(8,128)(2,1)}, u32[]{:S(2)}, u32[]{:S(2)}) collective-permute-start(bf16[2,384,768]{2,1,0:T(8,128)(2,1)S(1)} %bitcast.643), channel_id=1, source_target_pairs={{0,4},{1,5},{2,6},{3,7},{4,0},{5,1},{6,2},{7,3},{8,12},{9,13},{10,... | collective-permute-start | bytes 3538952 | tf_op jit(solution)/shard_map/ppermute | solution.py:66
  554.9 33.0 %collective-permute-start.42 = (bf16[224,4,192]{2,1,0:T(4,128)(2,1)S(1)}, bf16[224,4,192]{2,1,0:T(4,128)(2,1)S(1)}, u32[]{:S(2)}, u32[]{:S(2)}) collective-permute-start(bf16[224,4,192]{2,1,0:T(4,128)(2,1)S(1)} %pad_maximum_fusion.25), channel_id=1, source_target_pairs={{0,8},{1,9},{2,10},{3,11},{4,12},{5,13},{6,14},{7,15},{8,0},{9,1},... | collective-permute-start | bytes 1032200 | tf_op jit(solution)/shard_map/ppermute | solution.py:66
  601.3 39.8 %collective-permute-start.47 = (bf16[1,2,4,3,16,768]{5,4,3,1,2,0:T(8,128)(2,1)S(1)}, bf16[1,2,4,3,16,768]{5,4,3,1,2,0:T(8,128)(2,1)S(1)}, u32[]{:S(2)}, u32[]{:S(2)}) collective-permute-start(bf16[1,2,4,3,16,768]{5,4,3,1,2,0:T(8,128)(2,1)S(1)} %slice_bitcast_fusion.16), channel_id=1, source_target_pairs={{0,16},{1,17},{2,18},{3,19},{4,20},{5,21},{6,22},{7,23},{8,24},{9,... | collective-permute-start | bytes 1769480 | tf_op jit(solution)/shard_map/ppermute | solution.py:66
  625.6 45.6 %collective-permute-start.61 = (bf16[2,3,64,768]{3,2,1,0:T(8,128)(2,1)S(1)}, bf16[2,3,64,768]{3,2,1,0:T(8,128)(2,1)}, u32[]{:S(2)}, u32[]{:S(2)}) collective-permute-start(bf16[2,3,64,768]{3,2,1,0:T(8,128)(2,1)S(1)} %bitcast.688), channel_id=1, source_target_pairs={{0,4},{1,5},{2,6},{3,7},{4,0},{5,1},{6,2},{7,3},{8,12},{9,13},{10,... | collective-permute-start | bytes 1769480 | tf_op jit(solution)/shard_map/ppermute | solution.py:66
  (250 other events, 2207.3 us)

commit v2 on v1

v2 whole, which is shorter than its diff:
```python
import functools

import jax
import jax.numpy as jnp
from jax import lax
from jax.experimental import pallas as pl
from jax.experimental.pallas import tpu as pltpu
from jax.sharding import PartitionSpec as P

HEAD_DIM = 64
LAYERS = 2
PROMPTS = 50
QUARTERS = 4
PAD = 16
AXES = ("dp", "tensor")
epsilon = 1e-06
bf16 = jnp.bfloat16
f32 = jnp.float32
ANY = pl.BlockSpec(memory_space=pl.ANY)
SMEM = pl.BlockSpec(memory_space=pltpu.SMEM)
NEGATIVE = -1000000000.0


def nn(left, right):
    return lax.dot_general(left, right, (((1,), (0,)), ((), ())), preferred_element_type=f32)


def nt(left, right):
    return lax.dot_general(left, right, (((1,), (1,)), ((), ())), preferred_element_type=f32)


def turn(arr):
    return arr.astype(f32).T.astype(bf16)


def norm_parts(rows):
    centre = rows - jnp.mean(rows, axis=-1, keepdims=True)
    spread = jnp.mean(centre * centre, axis=-1, keepdims=True)
    scale = lax.rsqrt(spread + epsilon)
    return centre * scale, scale


def norm_back(hat, scale, gain, grad):
    inner = grad * gain
    along = jnp.mean(inner * hat, axis=-1, keepdims=True)
    return scale * (inner - jnp.mean(inner, axis=-1, keepdims=True) - hat * along)


def gate_pair(pre):
    size = jnp.abs(pre)
    t = 1.0 / (1.0 + 0.2316418882 * size)
    bell = jnp.exp(-0.5 * pre * pre)
    poly = 0.5307027145 * t - 0.7265760135
    poly = poly * t + 0.7107068705
    poly = poly * t - 0.142248368
    poly = poly * t + 0.127414796
    rest = poly * t * bell
    below = jnp.where(pre >= 0.0, 1.0 - rest, rest)
    return pre * below, below + pre * bell * 0.3989422804014327


def cost(flops, size, trans=0):
    return pl.CostEstimate(flops=flops, bytes_accessed=size, transcendentals=trans)


def params(mib):
    return pltpu.CompilerParams(vmem_limit_bytes=mib << 20)


def fetch(copies, sems, first=0):
    made = [pltpu.make_async_copy(src, dst, sems.at[first + i]) for i, (src, dst) in enumerate(copies)]
    for copy in made:
        copy.start()
    for copy in made:
        copy.wait()


def rows16(start, size):
    return pl.ds(pl.multiple_of(start, 16), size)


def attn_fetch(info, own_qkv, own_out, near, far, w_qkv, w_out, sems):
    rows_in, rows_out = own_qkv.shape[0], own_out.shape[0]
    part_in, part_out = rows_in // QUARTERS, rows_out // QUARTERS

    def pieces(bufs, block):
        copies = []
        for i in range(QUARTERS):
            quarter = info[2 + i]
            src = bufs[i]
            copies.append(
                (
                    src.at[pl.ds(0, part_in)],
                    w_qkv.at[rows16(block * rows_in + part_in * quarter, part_in)],
                )
            )
            copies.append(
                (
                    src.at[pl.ds(part_in, part_out)],
                    w_out.at[rows16(block * rows_out + part_out * quarter, part_out)],
                )
            )
        return copies

    @pl.when(info[0] == 0)
    def _():
        own = [
            (own_qkv, w_qkv.at[pl.ds(0, rows_in)]),
            (own_out, w_out.at[pl.ds(0, rows_out)]),
        ]
        fetch(own + pieces(near, 1), sems)

    @pl.when(info[0] != 0)
    def _():
        fetch(pieces(far, 0) + pieces(near, 1), sems)


def mlp_fetch(info, own_up, own_down, bufs, w_up, w_down, sems):
    width = own_up.shape[0]
    half = own_up.shape[1] // 2
    wide, tall = width // QUARTERS, half // QUARTERS
    split = width // 2
    start = info[0] * half
    copies = [
        (own_up.at[:, pl.ds(pl.multiple_of(start, 128), half)], w_up.at[:, pl.ds(0, half)]),
        (own_down.at[rows16(start, half)], w_down.at[pl.ds(0, half)]),
    ]
    for i in range(QUARTERS):
        quarter = info[2 + i]
        for k in range(bufs[i].shape[0]):
            src = bufs[i].at[k]
            units = rows16((k + 1) * half + tall * quarter, tall)
            copies.append(
                (
                    src.at[pl.ds(0, wide)],
                    w_up.at[rows16(wide * quarter, wide), pl.ds((k + 1) * half, half)],
                )
            )
            copies.append((src.at[pl.ds(wide, tall)], w_down.at[units, pl.ds(0, split)]))
            copies.append((src.at[pl.ds(wide + tall, tall)], w_down.at[units, pl.ds(split, split)]))
    fetch(copies, sems)


def head_masks(rows, cols, axis):
    place = lax.broadcasted_iota(jnp.int32, (rows, cols), axis)
    return place < HEAD_DIM


def attn_forward_kernel(later, info, *refs):
    if later:
        x_ref, own_ref, oth_ref = refs[:3]
        refs = refs[3:]
    else:
        x_ref = refs[0]
        refs = refs[1:]
    placed_ref, vec_ref, row_ref, own_qkv, own_out = refs[:5]
    near, far = refs[5:9], refs[9:13]
    xp_ref, a_ref, qkv_ref, mix_ref, lse_ref, part_ref = refs[13:19]
    w_qkv, w_out, sems = refs[19:]
    step = pl.program_id(0)

    @pl.when(step == 0)
    def _():
        attn_fetch(info, own_qkv, own_out, near, far, w_qkv, w_out, sems)

    rows = x_ref[0].astype(f32)
    if later:
        rows = rows + (own_ref[0].astype(f32) + oth_ref[0].astype(f32) + vec_ref[2:3, :])
    top = placed_ref.shape[1]
    place = lax.broadcasted_iota(jnp.int32, (top, rows.shape[1]), 0)
    here = (place >= 1) & (place <= PROMPTS)
    rows = jnp.concatenate(
        [jnp.where(here, placed_ref[0].astype(f32), rows[:top]), rows[top:]], axis=0
    )
    xp_ref[0] = rows
    hat, _ = norm_parts(rows)
    normed = (hat * vec_ref[0:1, :] + vec_ref[1:2, :]).astype(bf16)
    a_ref[0] = normed
    qkv = (nt(normed, w_qkv[...]) + row_ref[0:1, :]) * row_ref[1:2, :]
    seq = rows.shape[0]
    low = head_masks(seq, 128, 1)
    low_t = head_masks(128, seq, 0)
    count = info[6 + step]
    valid = lax.broadcasted_iota(jnp.int32, (seq, seq), 0) < count
    pairs = w_out.shape[0] // 128
    for p in range(pairs):
        blocks = [qkv[:, 384 * p + 128 * j : 384 * p + 128 * (j + 1)] for j in range(3)]
        query = jnp.where(low, blocks[0], blocks[1]).astype(bf16)
        key = pltpu.roll(jnp.where(low, blocks[2], blocks[0]), HEAD_DIM, 1).astype(bf16)
        value_t = jnp.where(low, blocks[1], blocks[2])
        qkv_ref[0, :, 384 * p : 384 * p + 128] = query
        qkv_ref[0, :, 384 * p + 128 : 384 * p + 256] = key
        qkv_ref[0, :, 384 * p + 256 : 384 * p + 384] = value_t.astype(bf16)
        value_t = value_t.T.astype(bf16)
        outs = []
        for h in range(2):
            mine = low if h == 0 else jnp.logical_not(low)
            one_key = jnp.where(mine, key, jnp.zeros_like(key))
            scores = jnp.where(valid, nt(one_key, query), NEGATIVE)
            peak = jnp.max(scores, axis=0, keepdims=True)
            exps = jnp.exp(scores - peak)
            total = jnp.sum(exps, axis=0, keepdims=True)
            lse_ref[0, 2 * p + h : 2 * p + h + 1, :] = peak + jnp.log(total)
            outs.append(nn(value_t, exps.astype(bf16)) * (1.0 / total))
        mixed = jnp.where(low_t, outs[0], outs[1]).T.astype(bf16)
        mix_ref[0, :, 128 * p : 128 * (p + 1)] = mixed
    part_ref[0] = nn(mix_ref[0], w_out[...]).astype(bf16)


def mlp_forward_kernel(info, xp_ref, own_ref, oth_ref, vec_ref, bias_ref, own_up, own_down, *refs):
    bufs = refs[:4]
    xm_ref, c_ref, act_ref, slope_ref, part_ref = refs[4:9]
    w_up, w_down, sems = refs[9:]

    @pl.when(pl.program_id(0) == 0)
    def _():
        mlp_fetch(info, own_up, own_down, bufs, w_up, w_down, sems)

    rows = xp_ref[0] + (own_ref[0].astype(f32) + oth_ref[0].astype(f32) + vec_ref[2:3, :])
    xm_ref[0] = rows
    hat, _ = norm_parts(rows)
    normed = (hat * vec_ref[0:1, :] + vec_ref[1:2, :]).astype(bf16)
    c_ref[0] = normed
    units = w_up.shape[1]
    for at in range(0, units, 384):
        pre = nn(normed, w_up[:, at : at + 384]) + bias_ref[:, at : at + 384]
        act, slope = gate_pair(pre)
        act_ref[0, :, at : at + 384] = act.astype(bf16)
        slope_ref[0, :, at : at + 384] = slope.astype(bf16)
    part_ref[0] = nn(act_ref[0], w_down[...]).astype(bf16)


def mlp_backward_kernel(masked, info, dx_ref, slope_ref, own_up, own_down, *refs):
    bufs = refs[:4]
    dz_ref, dh_ref, part_ref, sum_ref, upb_ref = refs[4:9]
    w_up, w_down, sems = refs[9:]
    step = pl.program_id(0)

    @pl.when(step == 0)
    def _():
        mlp_fetch(info, own_up, own_down, bufs, w_up, w_down, sems)
        sum_ref[...] = jnp.zeros_like(sum_ref)
        upb_ref[...] = jnp.zeros_like(upb_ref)

    grad = dx_ref[0].astype(f32)
    if masked:
        place = lax.broadcasted_iota(jnp.int32, grad.shape, 0)
        grad = jnp.where(place < info[6 + step], grad, 0.0)
    sum_ref[0:1, :] += jnp.sum(grad, axis=0, keepdims=True)
    low = grad.astype(bf16)
    dz_ref[0] = low
    units = w_up.shape[1]
    for at in range(0, units, 384):
        hidden = nt(low, w_down[at : at + 384, :]) * slope_ref[0, :, at : at + 384].astype(f32)
        hidden = hidden.astype(bf16)
        dh_ref[0, :, at : at + 384] = hidden
        upb_ref[0:1, at : at + 384] += jnp.sum(hidden.astype(f32), axis=0, keepdims=True)
    part_ref[0] = nt(dh_ref[0], w_up[...]).astype(bf16)


def mlp_weight_kernel(info, c_ref, dz_ref, act_ref, dh_ref, s1_ref, s2_ref, keep_ref, c_t, up, down):
    @pl.when(pl.program_id(0) == 0)
    def _():
        c_t[...] = turn(c_ref[...])

    up[...] = nn(c_t[...], dh_ref[...]).astype(bf16)
    down[...] = nn(turn(act_ref[...]), dz_ref[...]).astype(bf16)
    wide, tall = up.shape[0] // QUARTERS, down.shape[0] // QUARTERS
    split = down.shape[1] // 2
    for i, out in enumerate((keep_ref.at[0], s1_ref.at[0, 0], s2_ref.at[0], s1_ref.at[1, 0])):
        quarter = info[2 + i]
        out[0:wide, :] = up[rows16(wide * quarter, wide), :]
        rows = down[rows16(tall * quarter, tall), :]
        out[wide : wide + tall, :] = rows[:, :split]
        out[wide + tall :, :] = rows[:, split:]


def attn_backward_kernel(info, dx_ref, own_ref, oth_ref, xm_ref, vec_ref, qkv_ref, lse_ref, *refs):
    own_qkv, own_out = refs[:2]
    near, far = refs[2:6], refs[6:10]
    mid_ref, dy_ref, dqkv_ref, part_ref, sum_ref, pair_ref = refs[10:16]
    w_qkv, w_out, sems = refs[16:]
    step = pl.program_id(0)

    @pl.when(step == 0)
    def _():
        attn_fetch(info, own_qkv, own_out, near, far, w_qkv, w_out, sems)
        sum_ref[...] = jnp.zeros_like(sum_ref)
        pair_ref[...] = jnp.zeros_like(pair_ref)

    back = own_ref[0].astype(f32) + oth_ref[0].astype(f32)
    hat, scale = norm_parts(xm_ref[0])
    grad = dx_ref[0].astype(f32) + norm_back(hat, scale, vec_ref[0:1, :], back)
    mid_ref[0] = grad
    sum_ref[0:1, :] += jnp.sum(back * hat, axis=0, keepdims=True)
    sum_ref[1:2, :] += jnp.sum(back, axis=0, keepdims=True)
    sum_ref[2:3, :] += jnp.sum(grad, axis=0, keepdims=True)
    low_grad = grad.astype(bf16)
    dy_ref[0] = low_grad
    seq = grad.shape[0]
    d_mixed = nt(low_grad, w_out[...]).astype(bf16)
    low = head_masks(seq, 128, 1)
    low_t = head_masks(128, seq, 0)
    valid = lax.broadcasted_iota(jnp.int32, (seq, seq), 0) < info[6 + step]
    pairs = w_out.shape[0] // 128
    for p in range(pairs):
        query = qkv_ref[0, :, 384 * p : 384 * p + 128]
        key = qkv_ref[0, :, 384 * p + 128 : 384 * p + 256]
        value = qkv_ref[0, :, 384 * p + 256 : 384 * p + 384]
        grad_o = d_mixed[:, 128 * p : 128 * (p + 1)]
        key_t = turn(key)
        d_query, d_key, d_value = [], [], []
        for h in range(2):
            mine = low if h == 0 else jnp.logical_not(low)
            none = jnp.zeros_like(key)
            scores = jnp.where(valid, nt(jnp.where(mine, key, none), query), NEGATIVE)
            probs = jnp.exp(scores - lse_ref[0, 2 * p + h : 2 * p + h + 1, :])
            d_probs = nt(jnp.where(mine, value, none), grad_o)
            along = jnp.sum(probs * d_probs, axis=0, keepdims=True)
            d_scores = (probs * (d_probs - along)).astype(bf16)
            d_value.append(nn(probs.astype(bf16), grad_o))
            d_key.append(nn(d_scores, query))
            d_query.append(nn(key_t, d_scores))
        d_query = jnp.where(low_t, d_query[0], d_query[1]).T * (HEAD_DIM**-0.5)
        d_key = pltpu.roll(jnp.where(low, d_key[0], d_key[1]), HEAD_DIM, 1)
        d_value = jnp.where(low, d_value[0], d_value[1])
        for j, block in enumerate(
            (
                jnp.where(low, d_query, d_key),
                jnp.where(low, d_value, d_query),
                jnp.where(low, d_key, d_value),
            )
        ):
            block = block.astype(bf16)
            at = 384 * p + 128 * j
            dqkv_ref[0, :, at : at + 128] = block
            pair_ref[0:1, at : at + 128] += jnp.sum(block.astype(f32), axis=0, keepdims=True)
    part_ref[0] = nn(dqkv_ref[0], w_qkv[...]).astype(bf16)


def attn_weight_kernel(info, a_ref, dqkv_ref, dy_ref, mix_ref, s1_ref, s2_ref, keep_ref, w_in, w_out):
    for at in range(0, w_in.shape[0], 384):
        w_in[at : at + 384, :] = nn(turn(dqkv_ref[:, at : at + 384]), a_ref[...]).astype(bf16)
    w_out[...] = nn(turn(mix_ref[...]), dy_ref[...]).astype(bf16)
    rows_in, rows_out = w_in.shape[0] // 2, w_out.shape[0] // 2
    part_in, part_out = rows_in // QUARTERS, rows_out // QUARTERS
    for i, out in enumerate((keep_ref, s1_ref.at[0], s2_ref, s1_ref.at[1])):
        quarter = info[2 + i]
        for b in range(2):
            out[b, 0:part_in, :] = w_in[rows16(b * rows_in + part_in * quarter, part_in), :]
            out[b, part_in:, :] = w_out[rows16(b * rows_out + part_out * quarter, part_out), :]


def norm_backward_kernel(last, mid_ref, own_ref, oth_ref, xp_ref, vec_ref, dx_ref, at_ref, sum_ref):
    @pl.when(pl.program_id(0) == 0)
    def _():
        sum_ref[...] = jnp.zeros_like(sum_ref)

    back = own_ref[0].astype(f32) + oth_ref[0].astype(f32)
    hat, scale = norm_parts(xp_ref[0])
    grad = mid_ref[0] + norm_back(hat, scale, vec_ref[0:1, :], back)
    sum_ref[0:1, :] += jnp.sum(back * hat, axis=0, keepdims=True)
    sum_ref[1:2, :] += jnp.sum(back, axis=0, keepdims=True)
    top = at_ref.shape[1]
    place = lax.broadcasted_iota(jnp.int32, (top, grad.shape[1]), 0)
    here = (place >= 1) & (place <= PROMPTS)
    at_ref[0] = grad[:top]
    dx_ref[0, 0:top, :] = jnp.where(here, 0.0, grad[:top]).astype(dx_ref.dtype)
    dx_ref[0, top:, :] = grad[top:].astype(dx_ref.dtype)


def reversed_bits(value, bits):
    return sum(((value >> b) & 1) << (bits - 1 - b) for b in range(bits))


def xor_order(arr, axis, index, bits):
    for b in range(bits):
        shape = arr.shape
        split = shape[:axis] + (shape[axis] >> (b + 1), 2, 1 << b) + shape[axis + 1 :]
        parts = arr.reshape(split)
        arr = jnp.where(((index >> b) & 1) == 1, jnp.flip(parts, axis + 1), parts).reshape(shape)
    return arr


def build(dp_size, tensor_size):
    planes = dp_size // 2
    bits = planes.bit_length() - 1
    zbits = tensor_size.bit_length() - 1

    def send(arr, target):
        pairs = []
        for dp in range(dp_size):
            for z in range(tensor_size):
                to = target(dp >> 1, dp & 1, z)
                if to is not None:
                    plane, core, depth = to
                    pairs.append((dp * tensor_size + z, (plane * 2 + core) * tensor_size + depth))
        return lax.ppermute(arr, AXES, pairs)

    def other_core(p, c, z):
        return p, 1 - c, z

    def along(k):
        return lambda p, c, z: (p, c, z ^ k)

    def across(bit):
        return lambda p, c, z: (p ^ (1 << bit), c, z)

    def flip(step, only=None):
        def target(p, c, z):
            if only is not None and c != only:
                return None
            return p ^ (1 << ((1 - step) if c else step)), c, z

        return target

    def near_of(p, c, z):
        return p, c, z ^ (1 + c)

    def far_of(p, c, z):
        return (p, c, z ^ 3) if c else None

    def plane_gather(piece, only=None):
        one = send(piece, flip(0, only))
        two = send(piece, flip(1, only))
        return [piece, one, two, send(one, flip(1, only))]

    def plane_reduce(s1, s2, keep):
        got = send(s1, flip(0))
        two = (s2.astype(f32) + got[1].astype(f32)).astype(bf16)
        last = send(two, flip(1))
        return keep.astype(f32) + got[0].astype(f32) + last.astype(f32)

    def per_device(
        tokens,
        cotangent,
        task_ids,
        key_mask,
        prompts,
        norm_gain,
        norm_bias,
        qkv_weight,
        qv_bias,
        out_weight,
        branch_bias,
        up_weight,
        up_bias,
        down_weight,
    ):
        group, rows_local, width = tokens.shape
        images = group // 2
        seq = rows_local * tensor_size
        in_rows = qkv_weight.shape[2]
        heads = in_rows // (3 * HEAD_DIM)
        out_rows = heads * HEAD_DIM
        inner = 2 * out_rows
        hidden = up_weight.shape[2]
        half_units = hidden // 2
        units = half_units * tensor_size
        wide, tall = width // QUARTERS, half_units // QUARTERS
        task_count = prompts.shape[1]
        per_dev = task_count // dp_size
        place = lax.axis_index("dp")
        z = lax.axis_index("tensor")
        core = place & 1
        plane = place >> 1
        quarter = plane & 3
        first_core = core == 0
        odd = z & 1
        all_rows = images * seq
        top = 64

        def pick(arr, index, axis):
            return lax.dynamic_index_in_dim(arr, index, axis, keepdims=False)

        def cut(arr, start, size, axis):
            return lax.dynamic_slice_in_dim(arr, start, size, axis)

        def join(mine, theirs, axis):
            return jnp.where(
                first_core,
                jnp.concatenate([mine, theirs], axis),
                jnp.concatenate([theirs, mine], axis),
            )

        def gather_images(arr):
            one = cut(arr, odd * images, images, 0)
            two = cut(arr, (1 - odd) * images, images, 0)
            got_one = send(one, lambda p, c, d: (p, d >> 1, 2 * c + (d & 1)))
            got_two = send(two, lambda p, c, d: (p, d >> 1, 2 * c + 1 - (d & 1)))
            half = jnp.where(
                odd == 0,
                jnp.concatenate([got_one, got_two], 1),
                jnp.concatenate([got_two, got_one], 1),
            )
            return join(half, send(half, other_core), 1)

        def spread_images(rows_of):
            one = rows_of(rows_local * (2 * core + odd))
            two = rows_of(rows_local * (2 * core + 1 - odd))
            got_one = send(one, lambda p, c, d: (p, d >> 1, 2 * c + (d & 1)))
            got_two = send(two, lambda p, c, d: (p, d >> 1, 2 * c + 1 - (d & 1)))
            return jnp.where(
                odd == 0,
                jnp.concatenate([got_one, got_two], 0),
                jnp.concatenate([got_two, got_one], 0),
            )

        facts = jnp.concatenate([jnp.sum(key_mask, axis=1, keepdims=True), task_ids], axis=1)
        facts = cut(facts, odd * images, images, 0)
        facts = jnp.where(core == (z >> 1), facts, send(facts, other_core))
        counts, tasks = facts[:, 0], facts[:, 1:]
        ranks = [
            quarter ^ jnp.where(first_core, r, reversed_bits(r, 2)) for r in range(QUARTERS)
        ]
        info = jnp.concatenate(
            [jnp.stack([core, z] + ranks), counts, jnp.zeros((16 - 6 - images,), jnp.int32)]
        ).astype(jnp.int32)

        gains = norm_gain.astype(f32)
        shifts = norm_bias.astype(f32)
        biases = branch_bias.astype(f32)

        def vec(*vectors):
            return jnp.pad(jnp.stack(vectors), ((0, 8 - len(vectors)), (0, 0)))

        own_qkv = [qkv_weight[layer].T for layer in range(LAYERS)]

        def attn_gather(layer):
            bias = jnp.pad(qv_bias[layer][None], ((0, PAD - 1), (0, width - qv_bias.shape[1])))
            piece = jnp.concatenate(
                [
                    cut(own_qkv[layer], quarter * (in_rows // 4), in_rows // 4, 0),
                    cut(out_weight[layer], quarter * (out_rows // 4), out_rows // 4, 0),
                    bias,
                ],
                axis=0,
            )
            near = plane_gather(send(piece, near_of))
            far = plane_gather(send(piece, far_of), only=1)
            size = qv_bias.shape[1]
            last = in_rows // 4 + out_rows // 4
            near_bias = near[0][last, :size]
            first_bias = jnp.where(first_core, qv_bias[layer], far[0][last, :size])
            pair = jnp.stack([first_bias, near_bias]).astype(f32)
            pair = pair.reshape(2 * heads, 2, HEAD_DIM)
            pair = jnp.stack([pair[:, 0], jnp.zeros_like(pair[:, 0]), pair[:, 1]], axis=1)
            scale = jnp.broadcast_to(
                jnp.array([HEAD_DIM**-0.5, 1.0, 1.0], f32)[None, :, None], pair.shape
            )
            rows = vec(pair.reshape(-1), scale.reshape(-1))
            return near, far, rows

        def mlp_gather(layer):
            bias = jnp.pad(up_bias[layer].reshape(2, half_units), ((0, PAD - 2), (0, 0)))
            mine = cut(down_weight[layer], core * half_units + quarter * tall, tall, 0)
            piece = jnp.concatenate(
                [
                    cut(
                        cut(up_weight[layer], quarter * wide, wide, 0),
                        core * half_units,
                        half_units,
                        1,
                    ),
                    mine[:, : width // 2],
                    mine[:, width // 2 :],
                    bias,
                ],
                axis=0,
            )
            got = [send(piece, along(k)) for k in range(1, tensor_size)]
            size = wide + 2 * tall
            bufs = plane_gather(jnp.stack([g[:size] for g in got]))
            rows = [pick(up_bias[layer].reshape(2, half_units), core, 0)]
            rows += [pick(g[size : size + 2], core, 0) for g in got]
            return bufs, jnp.concatenate(rows)[None].astype(f32)

        def image_block(size):
            return pl.BlockSpec((1, seq, size), lambda i: (i, 0, 0))

        def fixed(*shape):
            return pl.BlockSpec(shape, lambda i: (0,) * len(shape))

        def out_of(*shape, dtype=bf16):
            return jax.ShapeDtypeStruct(shape, dtype)

        rows_w, rows_w32 = out_of(images, seq, width), out_of(images, seq, width, dtype=f32)
        wide_block = image_block(width)
        attn_scratch = [
            pltpu.VMEM((2 * in_rows, width), bf16),
            pltpu.VMEM((inner, width), bf16),
            pltpu.SemaphoreType.DMA((16,)),
        ]
        mlp_scratch = [
            pltpu.VMEM((width, units), bf16),
            pltpu.VMEM((units, width), bf16),
            pltpu.SemaphoreType.DMA((2 + 12 * (tensor_size - 1),)),
        ]
        mm = 2 * all_rows * width
        heads_flops = 2 * images * 2 * heads * seq * seq * 128

        def attn_forward(layer, x, placed, vecs, rows, near, far):
            later = len(x) > 1
            return pl.pallas_call(
                functools.partial(attn_forward_kernel, later),
                grid=(images,),
                in_specs=[SMEM]
                + [wide_block] * len(x)
                + [pl.BlockSpec((1, top, width), lambda i: (i, 0, 0))]
                + [fixed(8, width), fixed(8, 2 * in_rows)]
                + [ANY] * 10,
                out_specs=[
                    wide_block,
                    wide_block,
                    image_block(2 * in_rows),
                    image_block(inner),
                    pl.BlockSpec((1, 8, seq), lambda i: (i, 0, 0)),
                    wide_block,
                ],
                out_shape=[
                    rows_w32,
                    rows_w,
                    out_of(images, seq, 2 * in_rows),
                    out_of(images, seq, inner),
                    out_of(images, 8, seq, dtype=f32),
                    rows_w,
                ],
                scratch_shapes=attn_scratch,
                compiler_params=params(40),
                cost_estimate=cost(mm * (3 * inner + inner) + 2 * heads_flops, 12 << 20, 1 << 20),
                name="attn_forward",
            )(info, *x, placed, vecs, rows, own_qkv[layer], out_weight[layer], *near, *far)

        def mlp_forward(layer, xp, own, oth, vecs, bias, bufs):
            return pl.pallas_call(
                mlp_forward_kernel,
                grid=(images,),
                in_specs=[SMEM]
                + [wide_block] * 3
                + [fixed(8, width), fixed(1, units)]
                + [ANY] * 6,
                out_specs=[wide_block, wide_block, image_block(units), image_block(units), wide_block],
                out_shape=[
                    rows_w32,
                    rows_w,
                    out_of(images, seq, units),
                    out_of(images, seq, units),
                    rows_w,
                ],
                scratch_shapes=mlp_scratch,
                compiler_params=params(48),
                cost_estimate=cost(mm * 2 * units, 18 << 20, 1 << 20),
                name="mlp_forward",
            )(info, xp, own, oth, vecs, bias, up_weight[layer], down_weight[layer], *bufs)

        def mlp_backward(layer, dx, slope, bufs):
            return pl.pallas_call(
                functools.partial(mlp_backward_kernel, dx.dtype == bf16),
                grid=(images,),
                in_specs=[SMEM, wide_block, image_block(units)] + [ANY] * 6,
                out_specs=[
                    wide_block,
                    image_block(units),
                    wide_block,
                    fixed(8, width),
                    fixed(8, units),
                ],
                out_shape=[
                    rows_w,
                    out_of(images, seq, units),
                    rows_w,
                    out_of(8, width, dtype=f32),
                    out_of(8, units, dtype=f32),
                ],
                scratch_shapes=mlp_scratch,
                compiler_params=params(48),
                cost_estimate=cost(mm * 2 * units, 16 << 20),
                name="mlp_backward",
            )(info, dx, slope, up_weight[layer], down_weight[layer], *bufs)

        piece_rows = wide + 2 * tall

        def mlp_weights(c, dz, act, dh):
            flat = lambda arr: arr.reshape(all_rows, arr.shape[2])
            by_shard = pl.BlockSpec((all_rows, half_units), lambda k: (0, k))
            return pl.pallas_call(
                mlp_weight_kernel,
                grid=(tensor_size,),
                in_specs=[SMEM, fixed(all_rows, width), fixed(all_rows, width), by_shard, by_shard],
                out_specs=[
                    pl.BlockSpec((2, 1, piece_rows, half_units), lambda k: (0, k, 0, 0)),
                    pl.BlockSpec((1, piece_rows, half_units), lambda k: (k, 0, 0)),
                    pl.BlockSpec((1, piece_rows, half_units), lambda k: (k, 0, 0)),
                ],
                out_shape=[
                    out_of(2, tensor_size, piece_rows, half_units),
                    out_of(tensor_size, piece_rows, half_units),
                    out_of(tensor_size, piece_rows, half_units),
                ],
                scratch_shapes=[
                    pltpu.VMEM((width, all_rows), bf16),
                    pltpu.VMEM((width, half_units), bf16),
                    pltpu.VMEM((half_units, width), bf16),
                ],
                compiler_params=params(40),
                cost_estimate=cost(mm * 2 * units, 14 << 20),
                name="mlp_weights",
            )(info, flat(c), flat(dz), flat(act), flat(dh))

        def attn_backward(layer, dx, own, oth, xm, vecs, qkv, lse, near, far):
            return pl.pallas_call(
                attn_backward_kernel,
                grid=(images,),
                in_specs=[SMEM]
                + [wide_block] * 4
                + [fixed(8, width), image_block(2 * in_rows)]
                + [pl.BlockSpec((1, 8, seq), lambda i: (i, 0, 0))]
                + [ANY] * 10,
                out_specs=[
                    wide_block,
                    wide_block,
                    image_block(2 * in_rows),
                    wide_block,
                    fixed(8, width),
                    fixed(8, 2 * in_rows),
                ],
                out_shape=[
                    rows_w32,
                    rows_w,
                    out_of(images, seq, 2 * in_rows),
                    rows_w,
                    out_of(8, width, dtype=f32),
                    out_of(8, 2 * in_rows, dtype=f32),
                ],
                scratch_shapes=attn_scratch,
                compiler_params=params(40),
                cost_estimate=cost(mm * (3 * inner + inner) + 5 * heads_flops, 15 << 20, 1 << 20),
                name="attn_backward",
            )(
                info, dx, own, oth, xm, vecs, qkv, lse,
                own_qkv[layer], out_weight[layer], *near, *far,
            )

        attn_rows = in_rows // 4 + out_rows // 4

        def attn_weights(a, dqkv, dy, mixed):
            flat = lambda arr: arr.reshape(all_rows, arr.shape[2])
            whole = pl.BlockSpec(memory_space=pltpu.VMEM)
            return pl.pallas_call(
                attn_weight_kernel,
                in_specs=[SMEM] + [whole] * 4,
                out_specs=[whole] * 3,
                out_shape=[
                    out_of(2, 2, attn_rows, width),
                    out_of(2, attn_rows, width),
                    out_of(2, attn_rows, width),
                ],
                scratch_shapes=[
                    pltpu.VMEM((2 * in_rows, width), bf16),
                    pltpu.VMEM((inner, width), bf16),
                ],
                compiler_params=params(40),
                cost_estimate=cost(mm * (3 * inner + inner), 10 << 20),
                name="attn_weights",
            )(info, flat(a), flat(dqkv), flat(dy), flat(mixed))

        def norm_backward(last, mid, own, oth, xp, vecs):
            return pl.pallas_call(
                functools.partial(norm_backward_kernel, last),
                grid=(images,),
                in_specs=[wide_block] * 4 + [fixed(8, width)],
                out_specs=[
                    wide_block,
                    pl.BlockSpec((1, top, width), lambda i: (i, 0, 0)),
                    fixed(8, width),
                ],
                out_shape=[
                    rows_w if last else rows_w32,
                    out_of(images, top, width, dtype=f32),
                    out_of(8, width, dtype=f32),
                ],
                compiler_params=params(32),
                cost_estimate=cost(20 * all_rows * width, 9 << 20),
                name="norm_backward",
            )(mid, own, oth, xp, vecs)

        tok = gather_images(tokens)
        placed = [
            jnp.pad(
                jnp.stack([pick(prompts[layer], tasks[i, layer], 0) for i in range(images)]),
                ((0, 0), (1, top - 1 - PROMPTS), (0, 0)),
            )
            for layer in range(LAYERS)
        ]
        attn_w = [attn_gather(layer) for layer in range(LAYERS)]
        mlp_w = [mlp_gather(layer) for layer in range(LAYERS)]
        kept = []
        x = (tok,)
        for layer in range(LAYERS):
            near, far, rows = attn_w[layer]
            bufs, up_row = mlp_w[layer]
            before = biases[layer - 1, 1]
            xp, a, qkv, mixed, lse, part = attn_forward(
                layer, x, placed[layer], vec(gains[layer, 0], shifts[layer, 0], before), rows, near, far
            )
            xm, c, act, slope, part_two = mlp_forward(
                layer, xp, part, send(part, other_core),
                vec(gains[layer, 1], shifts[layer, 1], biases[layer, 0]), up_row, bufs,
            )
            x = (xm, part_two, send(part_two, other_core))
            kept.append((xp, a, qkv, mixed, lse, xm, c, act, slope))

        def out_rows_at(start):
            rows, own, oth = (cut(arr, start, rows_local, 1).astype(f32) for arr in x)
            here = (start + jnp.arange(rows_local))[None, :] < counts[:, None]
            rows = rows + (own + oth + biases[LAYERS - 1, 1])
            return jnp.where(here[:, :, None], rows, 0.0).astype(bf16)

        out = spread_images(out_rows_at)

        dx = gather_images(cotangent)
        sums = [None] * LAYERS
        prompt_parts = [None] * LAYERS
        grads = [None] * LAYERS
        for layer in reversed(range(LAYERS)):
            xp, a, qkv, mixed, lse, xm, c, act, slope = kept[layer]
            near, far, _ = attn_w[layer]
            bufs, _ = mlp_w[layer]
            dz, dh, part, sum_mlp, upb = mlp_backward(layer, dx, slope, bufs)
            other = send(part, other_core)
            s1, s2, keep = mlp_weights(c, dz, act, dh)
            got = plane_reduce(s1, s2, keep)
            total = got[0]
            got = got.astype(bf16)
            for k in range(1, tensor_size):
                total = total + send(got[k], along(k)).astype(f32)
            for b in range(2, bits):
                total = total + send(total.astype(bf16), across(b)).astype(f32)
            mlp_all = lax.all_gather(total.astype(bf16), "dp", axis=0)[: 2 * QUARTERS]
            grad_in = dz if layer == LAYERS - 1 else dx
            mid, dy, dqkv, part, sum_attn, pair = attn_backward(
                layer, grad_in, part, other, xm, vec(gains[layer, 1]), qkv, lse, near, far
            )
            other = send(part, other_core)
            s1, s2, keep = attn_weights(a, dqkv, dy, mixed)
            got = plane_reduce(s1, s2, keep)
            low = got.astype(bf16)
            near_sum = send(low[1], near_of).astype(f32)
            far_sum = send(low[0], far_of).astype(f32)
            total = jnp.where(first_core, got[0], far_sum) + near_sum
            half = attn_rows // 2
            mine = jnp.where(first_core, total[:half], total[half:])
            theirs = jnp.where(first_core, total[half:], total[:half]).astype(bf16)
            total = mine + send(theirs, other_core).astype(f32)
            for b in range(2, bits):
                total = total + send(total.astype(bf16), across(b)).astype(f32)
            attn_all = lax.all_gather(total.astype(bf16), "dp", axis=0)[: 2 * QUARTERS]
            dx, at, sum_norm = norm_backward(
                layer == 0, mid, part, other, xp, vec(gains[layer, 0])
            )
            grads[layer] = (mlp_all, attn_all)
            norms = jnp.stack(
                [sum_norm[0], sum_attn[0], sum_norm[1], sum_attn[1], sum_attn[2], sum_mlp[0]]
            )
            sums[layer] = (norms, upb[0], pair[0])
            at = at[:, 1 : 1 + PROMPTS]
            owner = (plane ^ jnp.arange(planes)) * 2 + core
            task_list = owner[:, None] * per_dev + jnp.arange(per_dev)[None, :]
            hot = (task_list[:, :, None] == tasks[None, None, :, layer]).astype(f32)
            prompt_parts[layer] = sum(
                hot[:, :, i, None, None] * at[i][None, None] for i in range(images)
            ).reshape(planes, per_dev * PROMPTS, width)

        grad_tokens = spread_images(lambda start: cut(dx, start, rows_local, 1))

        norms = 0.5 * jnp.stack([s[0] for s in sums])
        shards = jnp.arange(tensor_size)
        hot = ((shards[:, None] ^ shards[None, :]) == z).astype(f32)
        upb = jnp.stack([s[1] for s in sums]).reshape(LAYERS, tensor_size, half_units)
        upb = jnp.einsum("sk,lkj->lsj", hot, upb, precision=lax.Precision.HIGHEST)
        upb = join(upb, jnp.zeros_like(upb), 2)
        pair = jnp.stack([s[2] for s in sums]).reshape(LAYERS, 2, heads, 3, HEAD_DIM)
        pair = jnp.stack([pair[:, :, :, 0], pair[:, :, :, 2]], axis=3)
        pair = pair.reshape(LAYERS, 2, heads * 2 * HEAD_DIM)
        index = jnp.stack([jnp.where(first_core, z, z ^ 3), z ^ (1 + core)])
        hot = (shards[:, None] == index[None, :]).astype(f32)
        pair = jnp.einsum("sb,lbj->lsj", hot, pair, precision=lax.Precision.HIGHEST)
        flat = jnp.concatenate([norms.reshape(-1), upb.reshape(-1), pair.reshape(-1)])
        flat = flat.reshape(-1, width)
        small_rows = flat.shape[0]
        flat = flat + send(flat.astype(bf16), other_core).astype(f32)
        wanted = jnp.concatenate(prompt_parts, axis=1).astype(bf16)
        for step in range(bits):
            pairs = wanted.reshape((wanted.shape[0] // 2, 2) + wanted.shape[1:])
            payload = jnp.concatenate([pairs[:, 1].reshape(-1, width), flat.astype(bf16)], axis=0)
            got = send(payload, across(step)).astype(f32)
            flat = flat.astype(bf16).astype(f32) + got[-small_rows:]
            wanted = (
                pairs[:, 0].astype(f32) + got[:-small_rows].reshape(pairs[:, 0].shape)
            ).astype(bf16)
        tail = jnp.concatenate([wanted[0].astype(f32), flat], axis=0)
        for step in range(zbits):
            tail = tail + send(tail.astype(bf16), along(1 << step)).astype(f32)
        block = width // tensor_size
        prompt_rows = LAYERS * per_dev * PROMPTS
        grad_prompts = cut(tail[:prompt_rows], z * block, block, 1)
        grad_prompts = grad_prompts.reshape(LAYERS, per_dev, PROMPTS, block)
        flat = tail[prompt_rows:].reshape(-1)
        sizes = [norms.size, norms.size + upb.size]
        norms = cut(flat[: sizes[0]].reshape(LAYERS, 3, 2, width), z * block, block, 3)
        grad_upb = pick(flat[sizes[0] : sizes[1]].reshape(LAYERS, tensor_size, hidden), z, 1)
        grad_pair = pick(flat[sizes[1] :].reshape(LAYERS, tensor_size, -1), z, 1)

        mlp_all = jnp.stack([g[0] for g in grads]).reshape(
            LAYERS, QUARTERS, 2, piece_rows, half_units
        )
        full_up = mlp_all[:, :, :, :wide].transpose(0, 1, 3, 2, 4).reshape(LAYERS, width, hidden)
        full_down = mlp_all[:, :, :, wide:].reshape(LAYERS, QUARTERS, 2, 2, tall, half_units)
        full_down = full_down.transpose(0, 2, 1, 4, 3, 5).reshape(LAYERS, hidden, width)
        attn_all = jnp.stack([g[1] for g in grads]).reshape(LAYERS, QUARTERS, attn_rows, width)
        full_qkv = attn_all[:, :, : in_rows // 4].reshape(LAYERS, in_rows, width).swapaxes(1, 2)
        full_out = attn_all[:, :, in_rows // 4 :].reshape(LAYERS, out_rows, width)
        return (
            out,
            grad_tokens,
            grad_prompts,
            norms[:, 0],
            norms[:, 1],
            full_qkv.astype(f32),
            grad_pair,
            full_out.astype(f32),
            norms[:, 2],
            full_up.astype(f32),
            grad_upb,
            full_down.astype(f32),
        )

    return per_device


def solution(mesh):
    placed = (
        P("dp", "tensor", None),
        P("dp", "tensor", None),
        P("dp", None),
        P("dp", None),
        P(),
        P(),
        P(),
        P(None, None, "tensor"),
        P(None, "tensor"),
        P(None, "tensor", None),
        P(),
        P(None, None, "tensor"),
        P(None, "tensor"),
        P(None, "tensor", None),
    )
    return jax.shard_map(
        build(mesh.shape["dp"], mesh.shape["tensor"]),
        mesh=mesh,
        in_specs=placed,
        out_specs=(
            P("dp", "tensor", None),
            P("dp", "tensor", None),
            P(None, "dp", None, "tensor"),
            P(None, None, "tensor"),
            P(None, None, "tensor"),
            P(None, None, "tensor"),
            P(None, "tensor"),
            P(None, "tensor", None),
            P(None, None, "tensor"),
            P(None, None, "tensor"),
            P(None, "tensor"),
            P(None, "tensor", None),
        ),
        check_vma=False,
    )
```

time: 705 us -> 624 us (0.89)
  Pallas kernels: 0 us -> 124 us
  other arithmetic: 143 us -> 45.8 us
  matrix products: 93 us -> 1.69 us
  waiting for transfers between devices: 152 us -> 217 us
  local copies, waits for them, and re-layouts: 169 us -> 113 us
  blocking collectives: 22.2 us -> 0 us
  starting transfers between devices: 101 us -> 87.6 us
  between operations: 16.4 us -> 27.4 us
    pallas_call x0 -> x14, Pallas kernels: none -> 124 us  [the longest x2 29.9 us: attn_backward(): pl.pallas_call(attn_backward_kernel, grid=(images,), in_specs=[SMEM] + [w...]
    dot_general x36 -> x2, matrix products: 93 us -> 1.69 us  [the longest x1 1.56 us: per_device(): pair = jnp.einsum('sb,lbj->lsj', hot, pair, precision=lax.Precision.HIGHEST)]
    ppermute x78 -> x72, waiting for transfers between devices: 152 us -> 217 us  [send(): return lax.ppermute(arr, AXES, pairs)]
    reshape x29 -> x11, local copies, waits for them, and re-layouts: 44.3 us -> 3.63 us  [the longest x1 0.76 us: per_device(): grad_prompts = grad_prompts.reshape(LAYERS, per_dev, PROMPTS, block)]
    reduce_sum x20 -> x1, other arithmetic: 34.9 us -> 0.12 us  [per_device(): jnp.sum(key_mask, axis=1, keepdims=True)]
    all_gather x1 -> x0, blocking collectives: 22.2 us -> none  [per_device(): bias_all = lax.all_gather(bias_pack, 'tensor', axis=0)]
    convert_element_type x6, local copies, waits for them, and re-layouts: 3.06 us -> 24.3 us  [the longest x2 13 us: per_device(): full_up.astype(f32)]
    slice x51 -> x35, local copies, waits for them, and re-layouts: 27.6 us -> 10.7 us  [the longest x8 2.1 us: mlp_gather(): rows += [pick(g[size:size + 2], core, 0) for g in got]]
  transfers between devices with their start and end apart: 78 -> 76, of which waited for: 15 -> 29; matrix products, arithmetic and copies ran while one was open for 50% -> 15% of each run, Pallas kernels for 0% -> 14%
where the time goes in v2:
time: 624 us; the launch traced here: 617 us
  waiting for transfers between devices  217 us (35%)
  Pallas kernels  124 us (20%)
  local copies, waits for them, and re-layouts  113 us (18%)
  starting transfers between devices  87.6 us (14%)
  other arithmetic  45.8 us (7%)
  between operations  27.4 us (4%)
    ppermute x72, waiting for transfers between devices, send(): return lax.ppermute(arr, AXES, pairs)  217 us
    ppermute x72, starting transfers between devices, send(): return lax.ppermute(arr, AXES, pairs)  87.4 us
    unnamed x252, local copies, waits for them, and re-layouts  37.4 us
    pallas_call x2, Pallas kernels, attn_backward(): pl.pallas_call(attn_backward_kernel, grid=(images,), in_specs=[SMEM] + [w...  29.9 us
    pallas_call x2, Pallas kernels, mlp_forward(): pl.pallas_call(mlp_forward_kernel, grid=(images,), in_specs=[SMEM] + [wid...  26.2 us
    pallas_call x2, Pallas kernels, attn_forward(): pl.pallas_call(functools.partial(attn_forward_kernel, later), grid=(image...  23.7 us
    pallas_call x2, Pallas kernels, mlp_backward(): pl.pallas_call(functools.partial(mlp_backward_kernel, dx.dtype == bf16),...  18.4 us
    pallas_call x2, Pallas kernels, mlp_weights(): pl.pallas_call(mlp_weight_kernel, grid=(tensor_size,), in_specs=[SMEM, fi...  15.1 us
  transfers between devices with their start and end apart: 76, of which 29 were waited for; matrix products, arithmetic and copies ran while one was open for 15% of the time, Pallas kernels for 14%

profile of v2, /device:TPU:0, one launch (start us, length us, event | category | flops | bytes accessed | tf_op | source)
XLA Modules:
  0.0 617.0 jit_solution(12477499266135458182)
XLA Ops:
  67.5 12.0 %collective-permute-done.14 = bf16[400,384]{1,0:T(8,128)(2,1)S(1)} collective-permute-done((bf16[400,384]{1,0:T(8,128)(2,1)}, bf16[400,384]{1,0:T(8,128)(2,1)S(1)}, u32[]{:S(2)}, u32[]{:S(2)}) %collective-permute-start.14) | collective-permute-done | bytes 307232 | tf_op jit(solution)/shard_map/ppermute | solution.py:398
  84.4 12.3 %collective-permute-done.5.refs_6_.refs_2_ = bf16[208,768]{1,0:T(8,128)(2,1)S(1)} collective-permute-done((bf16[208,768]{1,0:T(8,128)(2,1)}, bf16[208,768]{1,0:T(8,128)(2,1)S(1)}, u32[]{:S(2)}, u32[]{:S(2)}) %collective-permute-start.5) | collective-permute-done | bytes 319520 | tf_op jit(solution)/shard_map/ppermute | solution.py:398
  108.5 6.4 %collective-permute-done.8.refs_9_.refs_5_ = bf16[208,768]{1,0:T(8,128)(2,1)S(1)} collective-permute-done((bf16[208,768]{1,0:T(8,128)(2,1)S(1)}, bf16[208,768]{1,0:T(8,128)(2,1)S(1)}, u32[]{:S(2)}, u32[]{:S(2)}) %collective-permute-start.8) | collective-permute-done | bytes 319520 | tf_op jit(solution)/shard_map/ppermute | solution.py:398
  118.0 11.8 %attn_forward.2 = (f32[3,256,768]{2,1,0:T(8,128)S(1)}, bf16[3,256,768]{2,1,0:T(8,128)(2,1)S(1)}, bf16[3,256,1152]{2,1,0:T(8,128)(2,1)S(1)}, bf16[3,256,384]{2,1,...) custom-call(s32[16]{0:T(128)S(1)} %concatenate.100.info, ...), custom_call_target="tpu_custom_call" | custom-call | flops 2415919104 | bytes 12582912 | tf_op jit(solution)/shard_map/attn_forward/pallas_call | solution.py:604
  133.2 9.3 %collective-permute-start.12 = (bf16[3,256,768]{2,1,0:T(8,128)(2,1)}, bf16[3,256,768]{2,1,0:T(8,128)(2,1)}, u32[]{:S(2)}, u32[]{:S(2)}) collective-permute-start(bf16[3,256,768]{2,1,0:T(8,128)(2,1)} %get-tuple-element.75.own_ref), channel_id=1, source_target_pairs={{0,4},{1,5},{2,6},{3,7},{4,0},{5,1},{6,2},{7,3},{8,12},{9,13},{10,... | collective-permute-start | bytes 3538952 | tf_op jit(solution)/shard_map/ppermute | solution.py:398
  151.4 7.3 %collective-permute-done.17.refs_2_ = bf16[3,384,384]{2,1,0:T(8,128)(2,1)} collective-permute-done((bf16[3,384,384]{2,1,0:T(8,128)(2,1)}, bf16[3,384,384]{2,1,0:T(8,128)(2,1)}, u32[]{:S(2)}, u32[]{:S(2)}) %collective-permute-start.17) | collective-permute-done | bytes 884768 | tf_op jit(solution)/shard_map/ppermute | solution.py:398
  158.7 9.5 %collective-permute-done.18.refs_3_ = bf16[3,384,384]{2,1,0:T(8,128)(2,1)} collective-permute-done((bf16[3,384,384]{2,1,0:T(8,128)(2,1)}, bf16[3,384,384]{2,1,0:T(8,128)(2,1)}, u32[]{:S(2)}, u32[]{:S(2)}) %collective-permute-start.18) | collective-permute-done | bytes 884768 | tf_op jit(solution)/shard_map/ppermute | solution.py:398
  168.2 13.5 %mlp_forward.2 = (f32[3,256,768]{2,1,0:T(8,128)}, bf16[3,256,768]{2,1,0:T(8,128)(2,1)S(1)}, bf16[3,256,1536]{2,1,0:T(8,128)(2,1)}, bf16[3,256,1536]{2,1,0:T(8,128)(2,1)}, bf16[3,256,768]{2,1,0:T(8,128)(2,1)S(1)}) custom-call(s32[16]{0:T(128)S(1)} %concatenate.100.info, f32[3,256,768]{2,1,0:T(8,128)} %copy-done, ...), custom_call_target="tpu_custom_call" | custom-call | flops 3623878656 | bytes 18874368 | tf_op jit(solution)/shard_map/mlp_forward/pallas_call | solution.py:635
  188.0 6.2 %collective-permute-done.22.refs_9_.refs_3_ = bf16[208,768]{1,0:T(8,128)(2,1)S(1)} collective-permute-done((bf16[208,768]{1,0:T(8,128)(2,1)S(1)}, bf16[208,768]{1,0:T(8,128)(2,1)S(1)}, u32[]{:S(2)}, u32[]{:S(2)}) %collective-permute-start.22) | collective-permute-done | bytes 319520 | tf_op jit(solution)/shard_map/ppermute | solution.py:398
  197.6 9.4 %collective-permute-done.24.refs_11_.refs_5_ = bf16[208,768]{1,0:T(8,128)(2,1)S(1)} collective-permute-done((bf16[208,768]{1,0:T(8,128)(2,1)S(1)}, bf16[208,768]{1,0:T(8,128)(2,1)S(1)}, u32[]{:S(2)}, u32[]{:S(2)}) %collective-permute-start.24) | collective-permute-done | bytes 319520 | tf_op jit(solution)/shard_map/ppermute | solution.py:398
  207.9 11.9 %attn_forward.3 = (f32[3,256,768]{2,1,0:T(8,128)S(1)}, bf16[3,256,768]{2,1,0:T(8,128)(2,1)S(1)}, bf16[3,256,1152]{2,1,0:T(8,128)(2,1)S(1)}, bf16[3,256,384]{2,1,...) custom-call(s32[16]{0:T(128)S(1)} %concatenate.100.info, ...), custom_call_target="tpu_custom_call" | custom-call | flops 2415919104 | bytes 12582912 | tf_op jit(solution)/shard_map/attn_forward/pallas_call | solution.py:604
  222.9 7.5 %collective-permute-start.28 = (bf16[3,256,768]{2,1,0:T(8,128)(2,1)S(1)}, bf16[3,256,768]{2,1,0:T(8,128)(2,1)S(1)}, u32[]{:S(2)}, u32[]{:S(2)}) collective-permute-start(bf16[3,256,768]{2,1,0:T(8,128)(2,1)S(1)} %get-tuple-element.79.own_ref), channel_id=1, source_target_pairs={{0,4},{1,5},{2,6},{3,7},{4,0},{5,1},{6,2},{7,3},{8,12},{9,13},{10,... | collective-permute-start | bytes 3538952 | tf_op jit(solution)/shard_map/ppermute | solution.py:398
  236.3 7.2 %collective-permute-done.33.refs_2_ = bf16[3,384,384]{2,1,0:T(8,128)(2,1)S(1)} collective-permute-done((bf16[3,384,384]{2,1,0:T(8,128)(2,1)S(1)}, bf16[3,384,384]{2,1,0:T(8,128)(2,1)S(1)}, u32[]{:S(2)}, u32[]{:S(2)}) %collective-permute-start.33) | collective-permute-done | bytes 884768 | tf_op jit(solution)/shard_map/ppermute | solution.py:398
  243.5 9.5 %collective-permute-done.34.refs_3_ = bf16[3,384,384]{2,1,0:T(8,128)(2,1)S(1)} collective-permute-done((bf16[3,384,384]{2,1,0:T(8,128)(2,1)S(1)}, bf16[3,384,384]{2,1,0:T(8,128)(2,1)S(1)}, u32[]{:S(2)}, u32[]{:S(2)}) %collective-permute-start.34) | collective-permute-done | bytes 884768 | tf_op jit(solution)/shard_map/ppermute | solution.py:398
  254.0 12.6 %mlp_forward.3 = (f32[3,256,768]{2,1,0:T(8,128)}, bf16[3,256,768]{2,1,0:T(8,128)(2,1)S(1)}, bf16[3,256,1536]{2,1,0:T(8,128)(2,1)}, bf16[3,256,1536]{2,1,0:T(8,128)(2,1)}, bf16[3,256,768]{2,1,0:T(8,128)(2,1)S(1)}) custom-call(s32[16]{0:T(128)S(1)} %concatenate.100.info, f32[3,256,768]{2,1,0:T(8,128)} %copy-done.4, bf16[3,256,768]{2,1,0:T(8,128)(2,1)} %copy-done.47, ...), custom_call_target="tpu_custom_call" | custom-call | flops 3623878656 | bytes 18874368 | tf_op jit(solution)/shard_map/mlp_forward/pallas_call | solution.py:635
  268.6 8.5 %mlp_backward.2 = (bf16[3,256,768]{2,1,0:T(8,128)(2,1)S(1)}, bf16[3,256,1536]{2,1,0:T(8,128)(2,1)}, bf16[3,256,768]{2,1,0:T(8,128)(2,1)S(1)}, f32[8,768]{1,0:T(8,128)S(1)}, f32[8,1536]{1,0:T(8,128)S(1)}) custom-call(s32[16]{0:T(128)S(1)} %concatenate.100.info, bf16[3,256,768]{2,1,0:T(8,128)(2,1)} %maximum_select_fusion.1.dx_ref, ...), custom_call_target="tpu_custom_call" | custom-call | flops 3623878656 | bytes 16777216 | tf_op jit(solution)/shard_map/mlp_backward/pallas_call | solution.py:657
  283.8 14.5 %attn_backward.2 = (f32[3,256,768]{2,1,0:T(8,128)}, bf16[3,256,768]{2,1,0:T(8,128)(2,1)S(1)}, bf16[3,256,1152]{2,1,0:T(8,128)(2,1)S(1)}, bf16[3,256,768]{2,1,0:T...) custom-call(s32[16]{0:T(128)S(1)} %concatenate.100.info, bf16[3,256,768]{2,1,0:T(8,128)(2,1)S(1)} %copy-done.63, ...), custom_call_target="tpu_custom_call" | custom-call | flops 3321888768 | bytes 15728640 | tf_op jit(solution)/shard_map/attn_backward/pallas_call | solution.py:711
  310.6 9.8 %mlp_backward.3 = (bf16[3,256,768]{2,1,0:T(8,128)(2,1)S(1)}, bf16[3,256,1536]{2,1,0:T(8,128)(2,1)}, bf16[3,256,768]{2,1,0:T(8,128)(2,1)S(1)}, f32[8,768]{1,0:T(8,128)S(1)}, f32[8,1536]{1,0:T(8,128)S(1)}) custom-call(s32[16]{0:T(128)S(1)} %concatenate.100.info, f32[3,256,768]{2,1,0:T(8,128)} %copy-done.6, bf16[3,256,1536]{2,1,0:T(8,128)(2,1)} %get-tuple-element.90.slope_ref, ...), custom_call_target="tpu_custom_call" | custom-call | flops 3623878656 | bytes 16777216 | tf_op jit(solution)/shard_map/mlp_backward/pallas_call | solution.py:657
  326.9 7.6 %mlp_weights.3 = (bf16[2,4,384,384]{3,2,1,0:T(8,128)(2,1)}, bf16[4,384,384]{2,1,0:T(8,128)(2,1)S(1)}, bf16[4,384,384]{2,1,0:T(8,128)(2,1)S(1)}) custom-call(s32[16]{0:T(128)S(1)} %concatenate.100.info, bf16[768,768]{1,0:T(8,128)(2,1)S(1)} %bitcast.310, bf16[768,768]{1,0:T(8,128)(2,1)S(1)} %bitcast.311, bf16[768,1536]{1,0:T(8,128)(2,1)S(1)} %bitcast.303, ...), custom_call_target="tpu_custom_call" | custom-call | flops 3623878656 | bytes 14680064 | tf_op jit(solution)/shard_map/mlp_weights/pallas_call | solution.py:686
  337.6 15.4 %attn_backward.3 = (f32[3,256,768]{2,1,0:T(8,128)S(1)}, bf16[3,256,768]{2,1,0:T(8,128)(2,1)S(1)}, bf16[3,256,1152]{2,1,0:T(8,128)(2,1)S(1)}, bf16[3,256,768]{2,1...) custom-call(s32[16]{0:T(128)S(1)} %concatenate.100.info, f32[3,256,768]{2,1,0:T(8,128)} %copy-done.6, ...), custom_call_target="tpu_custom_call" | custom-call | flops 3321888768 | bytes 15728640 | tf_op jit(solution)/shard_map/attn_backward/pallas_call | solution.py:711
  359.6 12.3 %collective-permute-done.60 = bf16[192,768]{1,0:T(8,128)(2,1)S(1)} collective-permute-done((bf16[192,768]{1,0:T(8,128)(2,1)S(1)}, bf16[192,768]{1,0:T(8,128)(2,1)S(1)}, u32[]{:S(2)}, u32[]{:S(2)}) %collective-permute-start.60) | collective-permute-done | bytes 294944 | tf_op jit(solution)/shard_map/ppermute | solution.py:398
  381.5 7.7 %collective-permute-done.53 = bf16[2,192,768]{2,1,0:T(8,128)(2,1)S(1)} collective-permute-done((bf16[2,192,768]{2,1,0:T(8,128)(2,1)S(1)}, bf16[2,192,768]{2,1,0:T(8,128)(2,1)S(1)}, u32[]{:S(2)}, u32[]{:S(2)}) %collective-permute-start.53) | collective-permute-done | bytes 589856 | tf_op jit(solution)/shard_map/ppermute | solution.py:398
  395.0 8.4 %collective-permute-done.55 = bf16[192,768]{1,0:T(8,128)(2,1)S(1)} collective-permute-done((bf16[192,768]{1,0:T(8,128)(2,1)S(1)}, bf16[192,768]{1,0:T(8,128)(2,1)S(1)}, u32[]{:S(2)}, u32[]{:S(2)}) %collective-permute-start.55) | collective-permute-done | bytes 294944 | tf_op jit(solution)/shard_map/ppermute | solution.py:398
  414.4 7.5 %mlp_weights.2 = (bf16[2,4,384,384]{3,2,1,0:T(8,128)(2,1)}, bf16[4,384,384]{2,1,0:T(8,128)(2,1)S(1)}, bf16[4,384,384]{2,1,0:T(8,128)(2,1)S(1)}) custom-call(s32[16]{0:T(128)S(1)} %concatenate.100.info, bf16[768,768]{1,0:T(8,128)(2,1)S(1)} %bitcast.306, bf16[768,768]{1,0:T(8,128)(2,1)S(1)} %bitcast.308, bf16[768,1536]{1,0:T(8,128)(2,1)S(1)} %bitcast.301, ...), custom_call_target="tpu_custom_call" | custom-call | flops 3623878656 | bytes 14680064 | tf_op jit(solution)/shard_map/mlp_weights/pallas_call | solution.py:686
  438.6 16.3 %collective-permute-done.70 = bf16[384,384]{1,0:T(8,128)(2,1)S(1)} collective-permute-done((bf16[384,384]{1,0:T(8,128)(2,1)S(1)}, bf16[384,384]{1,0:T(8,128)(2,1)S(1)}, u32[]{:S(2)}, u32[]{:S(2)}) %collective-permute-start.70) | collective-permute-done | bytes 294944 | tf_op jit(solution)/shard_map/ppermute | solution.py:398
  480.2 15.1 %collective-permute-done.63 = bf16[4,384,384]{2,1,0:T(8,128)(2,1)} collective-permute-done((bf16[4,384,384]{2,1,0:T(8,128)(2,1)}, bf16[4,384,384]{2,1,0:T(8,128)(2,1)}, u32[]{:S(2)}, u32[]{:S(2)}) %collective-permute-start.63) | collective-permute-done | bytes 1179680 | tf_op jit(solution)/shard_map/ppermute | solution.py:398
  509.4 17.1 %collective-permute-done.65 = bf16[384,384]{1,0:T(8,128)(2,1)S(1)} collective-permute-done((bf16[384,384]{1,0:T(8,128)(2,1)S(1)}, bf16[384,384]{1,0:T(8,128)(2,1)S(1)}, u32[]{:S(2)}, u32[]{:S(2)}) %collective-permute-start.65) | collective-permute-done | bytes 294944 | tf_op jit(solution)/shard_map/ppermute | solution.py:398
  529.0 6.3 %collective-permute-done.49 = bf16[124,768]{1,0:T(8,128)(2,1)S(1)} collective-permute-done((bf16[124,768]{1,0:T(8,128)(2,1)S(1)}, bf16[124,768]{1,0:T(8,128)(2,1)S(1)}, u32[]{:S(2)}, u32[]{:S(2)}) %collective-permute-start.49) | collective-permute-done | bytes 190496 | tf_op jit(solution)/shard_map/ppermute | solution.py:398
  542.0 7.3 %collective-permute-start.51 = (bf16[124,768]{1,0:T(8,128)(2,1)S(1)}, bf16[124,768]{1,0:T(8,128)(2,1)S(1)}, u32[]{:S(2)}, u32[]{:S(2)}) collective-permute-start(bf16[124,768]{1,0:T(8,128)(2,1)S(1)} %fusion.37), channel_id=1, source_target_pairs={{0,2},{1,3},{2,0},{3,1},{4,6},{5,7},{6,4},{7,5},{8,10},{9,11},{10,... | collective-permute-start | bytes 571400 | tf_op jit(solution)/shard_map/ppermute | solution.py:398
  556.5 18.7 %collective-permute-done.51 = bf16[124,768]{1,0:T(8,128)(2,1)S(1)} collective-permute-done((bf16[124,768]{1,0:T(8,128)(2,1)S(1)}, bf16[124,768]{1,0:T(8,128)(2,1)S(1)}, u32[]{:S(2)}, u32[]{:S(2)}) %collective-permute-start.51) | collective-permute-done | bytes 190496 | tf_op jit(solution)/shard_map/ppermute | solution.py:398
  592.0 7.2 %reshape.613 = f32[2,768,768]{2,1,0:T(8,128)} reshape(f32[2,4,192,2,384]{4,3,2,1,0:T(2,128)} %copy.44) | data formatting | bytes 9437184 | tf_op jit(solution)/shard_map/convert_element_type | solution.py:933
  603.1 7.2 %reshape.614 = f32[2,768,768]{2,1,0:T(8,128)} reshape(f32[2,2,4,96,2,384]{5,4,3,2,1,0:T(2,128)} %bitcast.315) | data formatting | bytes 9437184 | tf_op jit(solution)/shard_map/convert_element_type | solution.py:935
  (597 shorter events, 256.4 us)
Async XLA Ops:
  7.2 571.0 %all-gather.11.cloned.1.call-start = ((), (), s32[]{:S(2)}) async-start(), calls=%async_computation.1 | async-start | bytes 1327104 | tf_op jit(solution)/shard_map/all_gather | solution.py:857
  14.3 70.0 %collective-permute-start.21 = (bf16[208,768]{1,0:T(8,128)(2,1)}, bf16[208,768]{1,0:T(8,128)(2,1)S(1)}, u32[]{:S(2)}, u32[]{:S(2)}) collective-permute-start(bf16[208,768]{1,0:T(8,128)(2,1)} %fusion.32), channel_id=1, source_target_pairs={{0,1},{1,0},{2,3},{3,2},{4,6},{5,7},{6,4},{7,5},{8,9},{9,8},{10,11... | collective-permute-start | bytes 958472 | tf_op jit(solution)/shard_map/ppermute | solution.py:398
  17.3 62.2 %collective-permute-start.20 = (bf16[208,768]{1,0:T(8,128)(2,1)}, bf16[208,768]{1,0:T(8,128)(2,1)S(1)}, u32[]{:S(2)}, u32[]{:S(2)}) collective-permute-start(bf16[208,768]{1,0:T(8,128)(2,1)} %fusion.32), channel_id=1, source_target_pairs={{4,7},{5,6},{6,5},{7,4},{12,15},{13,14},{14,13},{15,12},{20,23},{2... | collective-permute-start | bytes 958472 | tf_op jit(solution)/shard_map/ppermute | solution.py:398
  18.8 26.0 %collective-permute-start = (s32[3,3]{0,1:T(4,128)}, s32[3,3]{0,1:T(4,128)}, u32[]{:S(2)}, u32[]{:S(2)}) collective-permute-start(s32[3,3]{0,1:T(4,128)} %constant_dynamic-slice_fusion.26), channel_id=1, source_target_pairs={{0,4},{1,5},{2,6},{3,7},{4,0},{5,1},{6,2},{7,3},{8,12},{9,13},{10,... | collective-permute-start | bytes 116 | tf_op jit(solution)/shard_map/ppermute | solution.py:398
  22.5 39.4 %collective-permute-start.2 = (bf16[3,64,768]{2,1,0:T(8,128)(2,1)}, bf16[3,64,768]{2,1,0:T(8,128)(2,1)}, u32[]{:S(2)}, u32[]{:S(2)}) collective-permute-start(bf16[3,64,768]{2,1,0:T(8,128)(2,1)} %get-tuple-element.213), channel_id=1, source_target_pairs={{0,1},{1,0},{2,5},{3,4},{4,3},{5,2},{6,7},{7,6},{8,9},{9,8},{10,13... | collective-permute-start | bytes 884744 | tf_op jit(solution)/shard_map/ppermute | solution.py:398
  23.0 40.5 %collective-permute-start.1 = (bf16[3,64,768]{2,1,0:T(8,128)(2,1)}, bf16[3,64,768]{2,1,0:T(8,128)(2,1)}, u32[]{:S(2)}, u32[]{:S(2)}) collective-permute-start(bf16[3,64,768]{2,1,0:T(8,128)(2,1)} %get-tuple-element.212), channel_id=1, source_target_pairs={{0,0},{1,1},{2,4},{3,5},{4,2},{5,3},{6,6},{7,7},{8,8},{9,9},{10,12... | collective-permute-start | bytes 884744 | tf_op jit(solution)/shard_map/ppermute | solution.py:398
  66.4 33.4 %collective-permute-start.3 = (bf16[3,128,768]{2,1,0:T(8,128)(2,1)S(1)}, bf16[3,128,768]{2,1,0:T(8,128)(2,1)}, u32[]{:S(2)}, u32[]{:S(2)}) collective-permute-start(bf16[3,128,768]{2,1,0:T(8,128)(2,1)S(1)} %maximum_select_fusion.2), channel_id=1, source_target_pairs={{0,4},{1,5},{2,6},{3,7},{4,0},{5,1},{6,2},{7,3},{8,12},{9,13},{10,... | collective-permute-start | bytes 1769480 | tf_op jit(solution)/shard_map/ppermute | solution.py:398
  82.8 63.1 %collective-permute-start.16 = (bf16[3,384,384]{2,1,0:T(8,128)(2,1)}, bf16[3,384,384]{2,1,0:T(8,128)(2,1)}, u32[]{:S(2)}, u32[]{:S(2)}) collective-permute-start(bf16[3,384,384]{2,1,0:T(8,128)(2,1)} %pad_maximum_fusion.1.refs_0_), channel_id=1, source_target_pairs={{0,8},{1,9},{2,10},{3,11},{4,20},{5,21},{6,22},{7,23},{8,0},{9,1},... | collective-permute-start | bytes 2654216 | tf_op jit(solution)/shard_map/ppermute | solution.py:398
  133.2 34.9 %collective-permute-start.12 = (bf16[3,256,768]{2,1,0:T(8,128)(2,1)}, bf16[3,256,768]{2,1,0:T(8,128)(2,1)}, u32[]{:S(2)}, u32[]{:S(2)}) collective-permute-start(bf16[3,256,768]{2,1,0:T(8,128)(2,1)} %get-tuple-element.75.own_ref), channel_id=1, source_target_pairs={{0,4},{1,5},{2,6},{3,7},{4,0},{5,1},{6,2},{7,3},{8,12},{9,13},{10,... | collective-permute-start | bytes 3538952 | tf_op jit(solution)/shard_map/ppermute | solution.py:398
  149.0 32.8 %collective-permute-start.31 = (bf16[400,384]{1,0:T(8,128)(2,1)}, bf16[400,384]{1,0:T(8,128)(2,1)}, u32[]{:S(2)}, u32[]{:S(2)}) collective-permute-start(bf16[400,384]{1,0:T(8,128)(2,1)} %fusion.35), channel_id=1, source_target_pairs={{0,3},{1,2},{2,1},{3,0},{4,7},{5,6},{6,5},{7,4},{8,11},{9,10},{10,... | collective-permute-start | bytes 921608 | tf_op jit(solution)/shard_map/ppermute | solution.py:398
  150.6 32.7 %collective-permute-start.30 = (bf16[400,384]{1,0:T(8,128)(2,1)}, bf16[400,384]{1,0:T(8,128)(2,1)}, u32[]{:S(2)}, u32[]{:S(2)}) collective-permute-start(bf16[400,384]{1,0:T(8,128)(2,1)} %fusion.35), channel_id=1, source_target_pairs={{0,2},{1,3},{2,0},{3,1},{4,6},{5,7},{6,4},{7,5},{8,10},{9,11},{10,... | collective-permute-start | bytes 921608 | tf_op jit(solution)/shard_map/ppermute | solution.py:398
  158.7 28.0 %collective-permute-start.29 = (bf16[400,384]{1,0:T(8,128)(2,1)}, bf16[400,384]{1,0:T(8,128)(2,1)S(1)}, u32[]{:S(2)}, u32[]{:S(2)}) collective-permute-start(bf16[400,384]{1,0:T(8,128)(2,1)} %fusion.35), channel_id=1, source_target_pairs={{0,1},{1,0},{2,3},{3,2},{4,5},{5,4},{6,7},{7,6},{8,9},{9,8},{10,11... | collective-permute-start | bytes 921608 | tf_op jit(solution)/shard_map/ppermute | solution.py:398
  181.7 26.1 %collective-permute-start.19 = (bf16[3,256,768]{2,1,0:T(8,128)(2,1)S(1)}, bf16[3,256,768]{2,1,0:T(8,128)(2,1)S(1)}, u32[]{:S(2)}, u32[]{:S(2)}) collective-permute-start(bf16[3,256,768]{2,1,0:T(8,128)(2,1)S(1)} %get-tuple-element.77.refs_1_), channel_id=1, source_target_pairs={{0,4},{1,5},{2,6},{3,7},{4,0},{5,1},{6,2},{7,3},{8,12},{9,13},{10,... | collective-permute-start | bytes 3538952 | tf_op jit(solution)/shard_map/ppermute | solution.py:398
  186.9 44.8 %collective-permute-start.32 = (bf16[3,384,384]{2,1,0:T(8,128)(2,1)S(1)}, bf16[3,384,384]{2,1,0:T(8,128)(2,1)S(1)}, u32[]{:S(2)}, u32[]{:S(2)}) collective-permute-start(bf16[3,384,384]{2,1,0:T(8,128)(2,1)S(1)} %pad_maximum_fusion.2.refs_0_), channel_id=1, source_target_pairs={{0,8},{1,9},{2,10},{3,11},{4,20},{5,21},{6,22},{7,23},{8,0},{9,1},... | collective-permute-start | bytes 2654216 | tf_op jit(solution)/shard_map/ppermute | solution.py:398
  197.5 34.9 %collective-permute-start.39 = (bf16[3,64,768]{2,1,0:T(8,128)(2,1)S(1)}, bf16[3,64,768]{2,1,0:T(8,128)(2,1)S(1)}, u32[]{:S(2)}, u32[]{:S(2)}) collective-permute-start(bf16[3,64,768]{2,1,0:T(8,128)(2,1)S(1)} %get-tuple-element.207), channel_id=1, source_target_pairs={{0,1},{1,0},{2,5},{3,4},{4,3},{5,2},{6,7},{7,6},{8,9},{9,8},{10,13... | collective-permute-start | bytes 884744 | tf_op jit(solution)/shard_map/ppermute | solution.py:398
  207.0 25.5 %collective-permute-start.38 = (bf16[3,64,768]{2,1,0:T(8,128)(2,1)S(1)}, bf16[3,64,768]{2,1,0:T(8,128)(2,1)S(1)}, u32[]{:S(2)}, u32[]{:S(2)}) collective-permute-start(bf16[3,64,768]{2,1,0:T(8,128)(2,1)S(1)} %get-tuple-element.206), channel_id=1, source_target_pairs={{0,0},{1,1},{2,4},{3,5},{4,2},{5,3},{6,6},{7,7},{8,8},{9,9},{10,12... | collective-permute-start | bytes 884744 | tf_op jit(solution)/shard_map/ppermute | solution.py:398
  222.9 30.1 %collective-permute-start.28 = (bf16[3,256,768]{2,1,0:T(8,128)(2,1)S(1)}, bf16[3,256,768]{2,1,0:T(8,128)(2,1)S(1)}, u32[]{:S(2)}, u32[]{:S(2)}) collective-permute-start(bf16[3,256,768]{2,1,0:T(8,128)(2,1)S(1)} %get-tuple-element.79.own_ref), channel_id=1, source_target_pairs={{0,4},{1,5},{2,6},{3,7},{4,0},{5,1},{6,2},{7,3},{8,12},{9,13},{10,... | collective-permute-start | bytes 3538952 | tf_op jit(solution)/shard_map/ppermute | solution.py:398
  322.6 34.9 %collective-permute-start.58 = (bf16[2,192,768]{2,1,0:T(8,128)(2,1)S(1)}, bf16[2,192,768]{2,1,0:T(8,128)(2,1)S(1)}, u32[]{:S(2)}, u32[]{:S(2)}) collective-permute-start(bf16[2,192,768]{2,1,0:T(8,128)(2,1)S(1)} %fusion.6), channel_id=1, source_target_pairs={{0,16},{1,17},{2,18},{3,19},{4,12},{5,13},{6,14},{7,15},{8,24},{9,... | collective-permute-start | bytes 1769480 | tf_op jit(solution)/shard_map/ppermute | solution.py:398
  336.5 54.8 %collective-permute-start.67 = (bf16[2,4,384,384]{3,2,1,0:T(8,128)(2,1)}, bf16[2,4,384,384]{3,2,1,0:T(8,128)(2,1)}, u32[]{:S(2)}, u32[]{:S(2)}) collective-permute-start(bf16[2,4,384,384]{3,2,1,0:T(8,128)(2,1)} %get-tuple-element.134), channel_id=1, source_target_pairs={{0,8},{1,9},{2,10},{3,11},{4,20},{5,21},{6,22},{7,23},{8,0},{9,1},... | collective-permute-start | bytes 7077896 | tf_op jit(solution)/shard_map/ppermute | solution.py:398
  380.7 197.5 %all-gather.9.cloned.1.call-start = ((), (), s32[]{:S(2)}) async-start(), calls=%async_computation | async-start | bytes 1327104 | tf_op jit(solution)/shard_map/all_gather | solution.py:857
  394.2 28.9 %collective-permute-start.68 = (bf16[4,384,384]{2,1,0:T(8,128)(2,1)}, bf16[4,384,384]{2,1,0:T(8,128)(2,1)}, u32[]{:S(2)}, u32[]{:S(2)}) collective-permute-start(bf16[4,384,384]{2,1,0:T(8,128)(2,1)} %fusion.1), channel_id=1, source_target_pairs={{0,16},{1,17},{2,18},{3,19},{4,12},{5,13},{6,14},{7,15},{8,24},{9,... | collective-permute-start | bytes 3538952 | tf_op jit(solution)/shard_map/ppermute | solution.py:398
  405.8 177.7 %all-gather.15.cloned.1.call-start = ((), (), s32[]{:S(2)}) async-start(), calls=%async_computation.3 | async-start | bytes 2654208 | tf_op jit(solution)/shard_map/all_gather | solution.py:839
  422.0 52.1 %collective-permute-start.62 = (bf16[2,4,384,384]{3,2,1,0:T(8,128)(2,1)}, bf16[2,4,384,384]{3,2,1,0:T(8,128)(2,1)}, u32[]{:S(2)}, u32[]{:S(2)}) collective-permute-start(bf16[2,4,384,384]{3,2,1,0:T(8,128)(2,1)} %get-tuple-element.128), channel_id=1, source_target_pairs={{0,8},{1,9},{2,10},{3,11},{4,20},{5,21},{6,22},{7,23},{8,0},{9,1},... | collective-permute-start | bytes 7077896 | tf_op jit(solution)/shard_map/ppermute | solution.py:398
  428.6 26.3 %collective-permute-start.70 = (bf16[384,384]{1,0:T(8,128)(2,1)S(1)}, bf16[384,384]{1,0:T(8,128)(2,1)S(1)}, u32[]{:S(2)}, u32[]{:S(2)}) collective-permute-start(bf16[384,384]{1,0:T(8,128)(2,1)S(1)} %get-tuple-element.184), channel_id=1, source_target_pairs={{0,2},{1,3},{2,0},{3,1},{4,6},{5,7},{6,4},{7,5},{8,10},{9,11},{10,... | collective-permute-start | bytes 884744 | tf_op jit(solution)/shard_map/ppermute | solution.py:398
  429.1 25.8 %collective-permute-start.69 = (bf16[384,384]{1,0:T(8,128)(2,1)S(1)}, bf16[384,384]{1,0:T(8,128)(2,1)S(1)}, u32[]{:S(2)}, u32[]{:S(2)}) collective-permute-start(bf16[384,384]{1,0:T(8,128)(2,1)S(1)} %get-tuple-element.182), channel_id=1, source_target_pairs={{0,1},{1,0},{2,3},{3,2},{4,5},{5,4},{6,7},{7,6},{8,9},{9,8},{10,11... | collective-permute-start | bytes 884744 | tf_op jit(solution)/shard_map/ppermute | solution.py:398
  432.4 35.4 %collective-permute-start.44 = (bf16[3,256,768]{2,1,0:T(8,128)(2,1)}, bf16[3,256,768]{2,1,0:T(8,128)(2,1)}, u32[]{:S(2)}, u32[]{:S(2)}) collective-permute-start(bf16[3,256,768]{2,1,0:T(8,128)(2,1)} %get-tuple-element.95.own_ref), channel_id=1, source_target_pairs={{0,4},{1,5},{2,6},{3,7},{4,0},{5,1},{6,2},{7,3},{8,12},{9,13},{10,... | collective-permute-start | bytes 3538952 | tf_op jit(solution)/shard_map/ppermute | solution.py:398
  456.8 126.6 %all-gather.13.cloned.1.call-start = ((), (), s32[]{:S(2)}) async-start(), calls=%async_computation.2 | async-start | bytes 2654208 | tf_op jit(solution)/shard_map/all_gather | solution.py:839
  478.6 23.4 %collective-permute-start.47 = (bf16[24,768]{1,0:T(8,128)(2,1)S(1)}, bf16[24,768]{1,0:T(8,128)(2,1)S(1)}, u32[]{:S(2)}, u32[]{:S(2)}) collective-permute-start(bf16[24,768]{1,0:T(8,128)(2,1)S(1)} %convert_element_type.387), channel_id=1, source_target_pairs={{0,4},{1,5},{2,6},{3,7},{4,0},{5,1},{6,2},{7,3},{8,12},{9,13},{10,... | collective-permute-start | bytes 110600 | tf_op jit(solution)/shard_map/ppermute | solution.py:398
  501.0 25.6 %collective-permute-start.65 = (bf16[384,384]{1,0:T(8,128)(2,1)S(1)}, bf16[384,384]{1,0:T(8,128)(2,1)S(1)}, u32[]{:S(2)}, u32[]{:S(2)}) collective-permute-start(bf16[384,384]{1,0:T(8,128)(2,1)S(1)} %get-tuple-element.187), channel_id=1, source_target_pairs={{0,2},{1,3},{2,0},{3,1},{4,6},{5,7},{6,4},{7,5},{8,10},{9,11},{10,... | collective-permute-start | bytes 884744 | tf_op jit(solution)/shard_map/ppermute | solution.py:398
  501.0 25.6 %collective-permute-start.64 = (bf16[384,384]{1,0:T(8,128)(2,1)S(1)}, bf16[384,384]{1,0:T(8,128)(2,1)S(1)}, u32[]{:S(2)}, u32[]{:S(2)}) collective-permute-start(bf16[384,384]{1,0:T(8,128)(2,1)S(1)} %get-tuple-element.185), channel_id=1, source_target_pairs={{0,1},{1,0},{2,3},{3,2},{4,5},{5,4},{6,7},{7,6},{8,9},{9,8},{10,11... | collective-permute-start | bytes 884744 | tf_op jit(solution)/shard_map/ppermute | solution.py:398
  502.1 25.5 %collective-permute-start.48 = (bf16[224,768]{1,0:T(8,128)(2,1)S(1)}, bf16[224,768]{1,0:T(8,128)(2,1)S(1)}, u32[]{:S(2)}, u32[]{:S(2)}) collective-permute-start(bf16[224,768]{1,0:T(8,128)(2,1)S(1)} %pad_maximum_fusion.5), channel_id=1, source_target_pairs={{0,8},{1,9},{2,10},{3,11},{4,12},{5,13},{6,14},{7,15},{8,0},{9,1},... | collective-permute-start | bytes 1032200 | tf_op jit(solution)/shard_map/ppermute | solution.py:398
  542.0 33.2 %collective-permute-start.51 = (bf16[124,768]{1,0:T(8,128)(2,1)S(1)}, bf16[124,768]{1,0:T(8,128)(2,1)S(1)}, u32[]{:S(2)}, u32[]{:S(2)}) collective-permute-start(bf16[124,768]{1,0:T(8,128)(2,1)S(1)} %fusion.37), channel_id=1, source_target_pairs={{0,2},{1,3},{2,0},{3,1},{4,6},{5,7},{6,4},{7,5},{8,10},{9,11},{10,... | collective-permute-start | bytes 571400 | tf_op jit(solution)/shard_map/ppermute | solution.py:398
  (168 other events, 1446.8 us)
Sparse Core Ops, SparseCore 0:
  380.9 24.9 all-gather.10
  407.7 25.7 all-gather.8
  457.0 28.8 all-gather.14
  527.6 28.0 all-gather.12
